TPU v7x, 128 devices: a whole 4x4x4 slice. The times are simulated.
128 devices in a mesh: grp: 2 (over y_hi), row: 8 (over x, core), col: 8 (over y_lo, z).
Axes of the slice: x: 4, y: 4 (y_hi: 2, y_lo: 2; y = y_hi * 2 + y_lo), z: 4, core: 2. Of those that a mesh axis runs over, the one named last changes fastest.
Arguments:
- child_update: bfloat16 [2, 7168, 1024], P('grp', ('row', 'col'))
- child_pivot: float32 [2, 1024, 1024], P('grp'), as said below
- child_map: int32 [2, 14], replicated, may hold values from 0 to 31, as said below
- parent_front: bfloat16 [16384, 16384], P('row', ('grp', 'col')), as said below
Outputs:
- front_out: float32 [16384, 16384], P('row', ('grp', 'col'))
Inputs may be any that keep to these rules, and one draw needn't show every extreme that they name: `child_map`: each row is strictly increasing, starts at 0 and ends at 31. `child_pivot`: each child's block is symmetric positive definite. `parent_front`: exactly symmetric; the parent front minus the two children's updates is positive definite.
All inputs are finite; a program needn't handle non-finite values.
Results may differ from a plain program's by a relative error of at most 0.0043.
Values may be sent and summed in bfloat16 or wider, within the bound.
A program may use at most 256 MiB of HBM per device.

v0:
```python
import jax
import jax.numpy as jnp
from jax import lax
from jax.sharding import PartitionSpec as P

TB = 512
PT = 32


def from_root(shard, axis, root):
    mine = lax.axis_index(axis) == root
    return lax.psum(jnp.where(mine, shard, jnp.zeros_like(shard)), axis)


def exact_nn(left_side, right_side):
    return jnp.dot(
        left_side, right_side, precision=lax.Precision.HIGHEST, preferred_element_type=jnp.float32
    )


def exact_nt(left_side, right_side):
    return lax.dot_general(
        left_side,
        right_side,
        (((1,), (1,)), ((), ())),
        precision=lax.Precision.HIGHEST,
        preferred_element_type=jnp.float32,
    )


def outer_sum(left_rows, right_rows):
    return lax.dot_general(
        left_rows, right_rows, (((1,), (1,)), ((), ())), preferred_element_type=jnp.float32
    )


def factor_pair(block):
    half = block.shape[0] // 2
    identity = jnp.eye(half, dtype=jnp.float32)
    first_factor = jnp.linalg.cholesky(block[:half, :half])
    first_inverse = lax.linalg.triangular_solve(first_factor, identity, left_side=True, lower=True)
    lower_left = exact_nt(block[half:, :half], first_inverse)
    second_factor = jnp.linalg.cholesky(block[half:, half:] - exact_nt(lower_left, lower_left))
    second_inverse = lax.linalg.triangular_solve(
        second_factor, identity, left_side=True, lower=True
    )
    inverse_left = -exact_nn(second_inverse, exact_nn(lower_left, first_inverse))
    zeros_block = jnp.zeros((half, half), jnp.float32)
    factor = jnp.concatenate(
        [
            jnp.concatenate([first_factor, zeros_block], axis=1),
            jnp.concatenate([lower_left, second_factor], axis=1),
        ],
        axis=0,
    )
    inverse = jnp.concatenate(
        [
            jnp.concatenate([first_inverse, zeros_block], axis=1),
            jnp.concatenate([inverse_left, second_inverse], axis=1),
        ],
        axis=0,
    )
    return (factor, inverse)


def locate_tiles(tile_map, parent_tiles):
    matches = tile_map[:, None] == jnp.arange(parent_tiles, dtype=jnp.int32)[None, :]
    positions = jnp.arange(tile_map.shape[0], dtype=jnp.int32)[:, None]
    inverse = jnp.sum(jnp.where(matches, positions, 0), axis=0)
    return (inverse, jnp.any(matches, axis=0))


def pick_rows(panel_tiles, inverse, present, first_tile, tile_count):
    chosen = lax.dynamic_slice_in_dim(inverse, first_tile, tile_count)
    wanted = lax.dynamic_slice_in_dim(present, first_tile, tile_count)
    picked = jnp.take(panel_tiles, chosen, axis=0)
    picked = jnp.where(wanted[:, None, None], picked, jnp.zeros_like(picked))
    return picked.reshape(tile_count * panel_tiles.shape[1], panel_tiles.shape[2])


def pick_sets(child_panel, tile_map, row_first, col_first, row_tiles, col_tiles, pivot_tiles):
    panel_tiles = child_panel.reshape(-1, TB, child_panel.shape[-1])
    inverse, present = locate_tiles(tile_map, PT)
    stripe = pick_rows(panel_tiles, inverse, present, row_first, row_tiles)
    across = pick_rows(panel_tiles, inverse, present, col_first, col_tiles)
    leading = pick_rows(panel_tiles, inverse, present, 0, pivot_tiles)
    return (stripe, across, leading)


def per_device(child_update, child_pivot, child_map, parent_front):
    width = child_pivot.shape[-1]
    stripe_rows, block_cols = parent_front.shape
    row_tiles = stripe_rows // TB
    col_tiles = block_cols // TB
    pivot_tiles = width // TB
    row_first = lax.axis_index("row") * row_tiles
    col_first = lax.axis_index(("grp", "col")) * col_tiles
    child_factor, child_inverse = factor_pair(child_pivot[0])
    local_panel = exact_nt(child_update[0].astype(jnp.float32), child_inverse).astype(jnp.bfloat16)
    gathered = lax.all_gather(local_panel[None], ("grp", "row", "col"), axis=1, tiled=True)
    both_panels = gathered.reshape(2, -1, width)
    first_sets = pick_sets(
        both_panels[0], child_map[0], row_first, col_first, row_tiles, col_tiles, pivot_tiles
    )
    second_sets = pick_sets(
        both_panels[1], child_map[1], row_first, col_first, row_tiles, col_tiles, pivot_tiles
    )
    stripe_both = jnp.concatenate([first_sets[0], second_sets[0]], axis=1)
    across_both = jnp.concatenate([first_sets[1], second_sets[1]], axis=1)
    leading_both = jnp.concatenate([first_sets[2], second_sets[2]], axis=1)
    column_panel = from_root(parent_front[:width], "row", 0)
    outgoing = jnp.concatenate([parent_front, column_panel], axis=0)
    incoming = from_root(outgoing, ("grp", "col"), 0)
    pivot_block = incoming[stripe_rows:].astype(jnp.float32) - outer_sum(leading_both, leading_both)
    stripe_block = incoming[:stripe_rows].astype(jnp.float32) - outer_sum(stripe_both, leading_both)
    cross_block = column_panel.astype(jnp.float32) - outer_sum(leading_both, across_both)
    pivot_factor, pivot_inverse = factor_pair(pivot_block)
    stripe_factor = exact_nt(stripe_block, pivot_inverse)
    cross_factor = exact_nn(pivot_inverse, cross_block)
    left_all = jnp.concatenate([stripe_both, stripe_factor.astype(jnp.bfloat16)], axis=1)
    right_all = jnp.concatenate(
        [across_both, jnp.transpose(cross_factor).astype(jnp.bfloat16)], axis=1
    )
    trailing = parent_front.astype(jnp.float32) - outer_sum(left_all, right_all)
    row_global = (
        lax.axis_index("row") * stripe_rows + jnp.arange(stripe_rows, dtype=jnp.int32)[:, None]
    )
    pivot_rows = row_global < width
    trailing = jnp.where(pivot_rows, jnp.float32(0.0), trailing)
    padded_pivot = jnp.pad(pivot_factor, ((0, stripe_rows - width), (0, 0)))
    panel_part = jnp.where(pivot_rows, padded_pivot, stripe_factor)
    first_block = lax.axis_index(("grp", "col")) == 0
    lead_cols = jnp.where(first_block, panel_part, trailing)
    return lead_cols


def solution(mesh):
    in_specs = (P("grp", ("row", "col"), None), P("grp", None, None), P(), P("row", ("grp", "col")))
    out_specs = P("row", ("grp", "col"))
    return jax.shard_map(
        per_device, mesh=mesh, in_specs=in_specs, out_specs=out_specs, check_vma=False
    )
```

profile of v0, /device:TPU:49, one launch (start us, length us, event | category | flops | bytes accessed | tf_op | source)
XLA Modules:
  0.0 1301.9 jit_solution(8584512899290143740)
XLA Ops:
  25.6 11.7 cholesky.462
  37.4 9.8 custom-call.35
  48.7 11.7 cholesky.481
  60.4 18.6 %custom-call.36 = f32[1,128,128]{1,2,0:T(8,128)S(1)} custom-call(f32[1,128,128]{2,1,0:T(8,128)S(1)} %get-tuple-element.133), custom_call_target="InvertDiagBlocksLowerTriangular" | custom-call | tf_op jit(solution)/shard_map/jit(cholesky)/cholesky | solution.py:40
  81.1 13.2 %cholesky.502 = f32[128,128]{1,0:T(8,128)} custom-call(f32[128,128]{1,0:T(8,128)} %cholesky.755), custom_call_target="Cholesky" | custom-call | tf_op jit(solution)/shard_map/jit(cholesky)/cholesky | solution.py:40
  96.4 11.3 custom-call.37
  109.1 11.7 cholesky.519
  125.3 8.1 while.8
  134.5 39.3 %custom-call.38 = f32[4,128,128]{1,2,0:T(8,128)S(1)} custom-call(f32[4,128,128]{2,1,0:T(8,128)S(1)} %get-tuple-element.35), custom_call_target="InvertDiagBlocksLowerTriangular" | custom-call | tf_op jit(solution)/shard_map/triangular_solve/custom-call.3 | solution.py:41
  191.0 11.7 cholesky.534
  203.9 10.0 custom-call.39
  217.8 11.7 cholesky.553
  231.5 9.8 custom-call.40
  245.2 13.2 %cholesky.574 = f32[128,128]{1,0:T(8,128)} custom-call(f32[128,128]{1,0:T(8,128)} %cholesky.768), custom_call_target="Cholesky" | custom-call | tf_op jit(solution)/shard_map/jit(cholesky)/cholesky | solution.py:43
  260.6 11.4 custom-call.41
  275.1 11.7 cholesky.591
  293.8 13.9 %while.9 = (s32[]{:T(128)}, f32[512,512]{1,0:T(8,128)}, s32[4,2]{0,1:T(2,128)S(1)}, f32[4,128,128]{2,1,0:T(8,128)}, s32[]{:T(128)}) while((s32[]{:T(128)}, f32[512,512]{1,0:T(8,128)}, s32[4,2]{0,1:T(2,128)S(1)}, f32[4,128,128]{2,1,0:T(8,128)}, s32[]{:T(128)}) %tuple.131), condition=%wide.while_cond.clone, body=%wide.while_body.clone.sunk | while | flops 2 | bytes 132705 | solution.py:44
  307.7 41.1 %custom-call.42 = f32[4,128,128]{1,2,0:T(8,128)} custom-call(f32[4,128,128]{2,1,0:T(8,128)} %get-tuple-element.36), custom_call_target="InvertDiagBlocksLowerTriangular" | custom-call | tf_op jit(solution)/shard_map/triangular_solve/custom-call.3 | solution.py:44
  376.5 383.1 %all-gather.3.cloned.1.call-done = bf16[14336,1024]{1,0:T(8,128)(2,1)} async-done(((bf16[112,1024]{1,0:T(8,128)(2,1)}), bf16[14336,1024]{1,0:T(8,128)(2,1)}) %all-gather.3.cloned.1.call-update) | async-done | bytes 29360144 | tf_op jit(solution)/shard_map/all_gather | solution.py:100
  759.7 22.0 %fusion.229 = (bf16[1,7168,1024]{2,1,0:T(8,128)(2,1)}, bf16[1,7168,1024]{2,1,0:T(8,128)(2,1)}) fusion(bf16[1,14336,1024]{2,1,0:T(8,128)(2,1)} %bitcast.223), kind=kLoop, calls=%fused_computation.396 | loop fusion | bytes 58720256 | tf_op jit(solution)/shard_map/slice | solution.py:103
  781.6 7.2 gather_fusion
  799.6 9.0 convert_subtract_fusion
  812.5 11.7 cholesky.606
  824.4 9.8 custom-call.43
  835.5 12.1 cholesky.625
  849.1 9.8 custom-call.44
  860.5 11.7 cholesky.646
  872.9 9.8 custom-call.45
  883.5 11.7 cholesky.663
  899.9 8.4 while.10
  909.3 39.3 %custom-call.46 = f32[4,128,128]{1,2,0:T(8,128)S(1)} custom-call(f32[4,128,128]{2,1,0:T(8,128)S(1)} %get-tuple-element.37), custom_call_target="InvertDiagBlocksLowerTriangular" | custom-call | tf_op jit(solution)/shard_map/triangular_solve/custom-call.3 | solution.py:41
  967.6 12.1 cholesky.678
  979.8 9.8 custom-call.47
  996.2 7.2 gather_fusion.4
  1010.4 11.7 cholesky.697
  1024.8 9.8 custom-call.48
  1037.9 11.9 cholesky.718
  1051.1 9.8 custom-call.49
  1063.1 11.7 cholesky.735
  1082.1 13.7 %while.11 = (s32[]{:T(128)}, f32[512,512]{1,0:T(8,128)}, s32[4,2]{0,1:T(2,128)S(1)}, f32[4,128,128]{2,1,0:T(8,128)}, s32[]{:T(128)}) while((s32[]{:T(128)}, f32[512,512]{1,0:T(8,128)}, s32[4,2]{0,1:T(2,128)S(1)}, f32[4,128,128]{2,1,0:T(8,128)}, s32[]{:T(128)}) %tuple.133), condition=%wide.while_cond.clone.2, body=%wide.while_body.clone.2.sunk | while | flops 2 | bytes 132705 | solution.py:44
  1095.8 40.9 %custom-call.50 = f32[4,128,128]{1,2,0:T(8,128)} custom-call(f32[4,128,128]{2,1,0:T(8,128)} %get-tuple-element.38), custom_call_target="InvertDiagBlocksLowerTriangular" | custom-call | tf_op jit(solution)/shard_map/triangular_solve/custom-call.3 | solution.py:44
  1146.3 8.0 gather_fusion.2
  1165.5 8.0 gather_fusion.3
  1188.1 14.9 %fusion.6 = f32[2048,1024]{0,1:T(8,128)} fusion(bf16[2048,1024]{0,1:T(8,128)(2,1)} %copy.48, bf16[2048,1024]{0,1:T(8,128)(2,1)} %copy.47, bf16[1024,1024]{1,0:T(8,128)(2,1)} %bitcast.234, bf16[1024,1024]{1,0:T(8,128)(2,1)} %bitcast.231), kind=kOutput, calls=%fused_computation.20 | convolution fusion | flops 8615100416 | bytes 20971520 | tf_op jit(solution)/shard_map/dot_general | solution.py:32
  1203.0 31.2 %fusion.232 = (bf16[2048,1024]{0,1:T(8,128)(2,1)}, f32[2048,1024]{0,1:T(8,128)}) fusion(f32[512,512]{1,0:T(8,128)S(1)} %copy-done.26, f32[128,512]{1,0:T(8,128)S(1)} %fusion.146, f32[128,512]{1,0:T(8,128)S(1)} %copy-done.17, f32[128,512]{1,0:T(8,128)S(1)} %copy-done.11, f32[128,512]{1,0:T(8,128)S(1)} %copy-done.4, ...), kind=kOutput, calls=%fused_computation.399 | convolution fusion | flops 25783435264 | bytes 28311552 | tf_op jit(solution)/shard_map/dot_general | solution.py:22
  1234.3 9.2 copy.40
  1254.6 18.1 %fusion.39 = bf16[1024,1024]{1,0:T(8,128)(2,1)} fusion(f32[1024,1024]{0,1:T(8,128)S(1)} %fusion.30, bf16[1024,1024]{0,1:T(8,128)(2,1)S(1)} %copy-done.18, f32[512,512]{1,0:T(8,128)S(1)} %copy-done.27, f32[128,512]{1,0:T(8,128)S(1)} %fusion.146, f32[128,512]{1,0:T(8,128)S(1)} %copy-done.17, f32[128,512]{1,0:T(8,128)S(1)} %copy-done.11, ...), kind=kOutput, calls=%fused_computation.68 | convolution fusion | flops 12895387648 | bytes 11534336 | tf_op jit(solution)/shard_map/dot_general | solution.py:16
  1272.8 21.5 %select_select_fusion = f32[2048,1024]{1,0:T(8,128)} fusion(bf16[2048,1024]{1,0:T(8,128)(2,1)} %param.14, f32[2048,1024]{1,0:T(8,128)} %copy.40, f32[1024,1024]{1,0:T(8,128)} %select_maximum_fusion.1, pred[2048]{0:T(1024)(128)(4,1)S(1)} %add_compare_fusion, pred[]{:T(512)S(6)} %eq.47, bf16[1024,1024]{1,0:T(8,128)(2,1)} %fusion.39, ...), kind=kOutput, calls=%fused_computation.24 | convolution fusion | flops 12952010752 | bytes 44042240 | tf_op jit(solution)/shard_map/dot_general | solution.py:32
  (298 shorter events, 254.4 us)
Async XLA Ops:
  7.4 354.4 %copy-start = (bf16[1,112,1024]{2,1,0:T(8,128)(2,1)S(1)}, bf16[1,112,1024]{2,1,0:T(8,128)(2,1)}, u32[]{:S(2)}) copy-start(bf16[1,112,1024]{2,1,0:T(8,128)(2,1)} %param.11) | copy-start | bytes 688132
  7.4 360.6 %all-reduce.8.cloned.1.call-start = ((), (), s32[]{:S(2)}) async-start(), calls=%async_computation | async-start | bytes 4194304 | tf_op jit(solution)/shard_map/psum | solution.py:12
  17.0 742.7 %all-gather.3.cloned.1.call-start = ((), (), s32[]{:S(2)}) async-start(), calls=%async_computation.2 | async-start | bytes 29589504 | tf_op jit(solution)/shard_map/all_gather | solution.py:100
  48.0 0.7 copy-start.32
  133.5 1.0 copy-start.12
  173.8 6.1 copy-start.2
  190.0 1.0 copy-start.15
  217.1 0.7 copy-start.30
  355.2 6.7 copy-start.28
  367.9 431.7 %all-reduce.10.cloned.1.call-start = ((), (), s32[]{:S(2)}) async-start(), calls=%async_computation.1 | async-start | bytes 12582912 | tf_op jit(solution)/shard_map/psum | solution.py:12
  374.9 0.7 copy-start.33
  808.6 2.0 copy-start.8
  834.8 0.7 copy-start.31
  908.4 1.0 copy-start.13
  948.6 6.1 copy-start.9
  966.6 1.0 copy-start.14
  996.2 14.2 %slice-start = ((f32[384,128]{1,0:T(8,128)}), f32[128,128]{1,0:T(8,128)S(1)}, s32[]{:S(2)}) async-start(f32[384,128]{1,0:T(8,128)} %convolution_subtract_fusion.14), calls=%async_computation.3 | async-start | bytes 131072 | tf_op jit(solution)/shard_map/jit(cholesky)/cholesky | solution.py:43
  996.2 25.9 %copy-start.29 = (f32[384,128]{1,0:T(8,128)S(1)}, f32[384,128]{1,0:T(8,128)}, u32[]{:S(2)}) copy-start(f32[384,128]{1,0:T(8,128)} %copy.33) | copy-start | bytes 589828
  1138.0 6.9 copy-start.3
  1140.6 4.4 copy-start.10
  1143.3 1.7 copy-start.16
  1178.2 6.6 copy-start.4
  1178.2 6.6 copy-start.11
  1178.2 6.6 copy-start.17
  1184.8 18.2 %slice-start.1 = ((s8[6291456]{0:T(1024)(128)(4,1)}), s8[4194304]{0:T(1024)(128)(4,1)S(1)}, s32[]{:S(2)}) async-start(s8[6291456]{0:T(1024)(128)(4,1)} %bitcast.240), calls=%async_computation.4 | async-start | bytes 8388608
  1188.1 14.9 %copy-start.24 = (f32[512,512]{1,0:T(8,128)}, f32[512,512]{1,0:T(8,128)S(1)}, u32[]{:S(2)}) copy-start(f32[512,512]{1,0:T(8,128)S(1)} %convolution_negate_fusion) | copy-start | bytes 3145732
  1188.1 14.9 %copy-start.26 = (f32[512,512]{1,0:T(8,128)S(1)}, f32[512,512]{1,0:T(8,128)}, u32[]{:S(2)}) copy-start(f32[512,512]{1,0:T(8,128)} %pad_maximum_fusion.5) | copy-start | bytes 3145732
  1188.1 14.9 %slice-start.2 = ((s8[6291456]{0:T(1024)(128)(4,1)}), s8[2097152]{0:T(1024)(128)(4,1)S(1)}, s32[]{:S(2)}) async-start(s8[6291456]{0:T(1024)(128)(4,1)} %bitcast.240), calls=%async_computation.5 | async-start | bytes 4194304
  1243.5 2.4 copy-start.19
  1243.5 2.9 copy-start.20
  1245.6 5.3 copy-start.21
  1245.9 5.0 copy-start.23
  1246.4 4.6 copy-start.5
  1246.4 4.6 copy-start.6
  1246.4 4.6 copy-start.7
  1250.9 2.7 copy-start.18
  1251.0 2.7 copy-start.25
  1251.0 3.7 copy-start.27
  1254.6 18.1 %copy-start.22 = (bf16[2,512,1024]{2,1,0:T(8,128)(2,1)S(1)}, bf16[2,512,1024]{2,1,0:T(8,128)(2,1)}, u32[]{:S(2)}) copy-start(bf16[2,512,1024]{2,1,0:T(8,128)(2,1)} %copy-done.21) | copy-start | bytes 6291460
  1272.8 21.5 %copy-start.1 = (bf16[1,112,1024]{2,1,0:T(8,128)(2,1)S(1)}, bf16[1,112,1024]{2,1,0:T(8,128)(2,1)}, u32[]{:S(2)}) copy-start(bf16[1,112,1024]{2,1,0:T(8,128)(2,1)} %param.11) | copy-start | bytes 688132
Sparse Core Ops, SparseCore 0:
  17.1 65.8 all-reduce.7
  375.1 130.0 all-reduce.9
Sparse Core Ops, SparseCore 1:
  367.9 391.7 all-gather.2
where the time goes:
time: 1310 us; the launch traced here: 1300 us
  other arithmetic  544 us (42%)
  waiting for transfers between devices  383 us (29%)
  matrix products  180 us (14%)
  local copies, waits for them, and re-layouts  168 us (13%)
  between operations  26.3 us (2%)
    all_gather x1, waiting for transfers between devices, per_device(): lax.all_gather(local_panel[None], ('grp', 'row', 'col'), axis=1, tiled=True)  383 us
    another operation x29, other arithmetic, factor_pair(): first_factor = jnp.linalg.cholesky(block[:half, :half])  171 us
    another operation x30, other arithmetic, factor_pair(): jnp.linalg.cholesky(block[half:, half:] - exact_nt(lower_left, lower_left))  166 us
    another operation x4, other arithmetic, factor_pair(): lax.linalg.triangular_solve(second_factor, identity, left_side=True, lowe...  87.2 us
    another operation x7, other arithmetic, factor_pair(): lax.linalg.triangular_solve(first_factor, identity, left_side=True, lower...  82.5 us
    dot_general x4, matrix products, outer_sum(): lax.dot_general(left_rows, right_rows, (((1,), (1,)), ((), ())), preferre...  49.9 us
    dot_general x6, matrix products, exact_nt(): lax.dot_general(left_side, right_side, (((1,), (1,)), ((), ())), precisio...  46.8 us
    gather x6, local copies, waits for them, and re-layouts, pick_rows(): picked = jnp.take(panel_tiles, chosen, axis=0)  42.1 us
  transfers between devices with their start and end apart: 3, of which 1 were waited for; matrix products, arithmetic and copies ran while one was open for 30% of the time, Pallas kernels for 0%

commit v1 on v0

v1 whole, which is shorter than its diff:
```python
import functools

import jax
import jax.numpy as jnp
from jax import lax
from jax.experimental import pallas as pl
from jax.experimental.pallas import tpu as pltpu
from jax.sharding import PartitionSpec as P

TB = 512
F32 = jnp.float32
BF16 = jnp.bfloat16
NB = 128
SUBS = 8
VM = pltpu.VMEM
NT = (((1,), (1,)), ((), ()))
NN = (((1,), (0,)), ((), ()))


CUT = 256


def dot16(a, b, dims=NN):
    return lax.dot_general(a, b, dims, preferred_element_type=F32)


def split(x):
    hi = x.astype(BF16)
    return hi, (x - hi.astype(F32)).astype(BF16)


def dot_nt(a, b):
    return lax.dot_general(
        a, b, NT, precision=lax.Precision.HIGHEST, preferred_element_type=F32
    )


def sum_products(x, y):
    terms = [a * b for a, b in zip(x, y)]
    while len(terms) > 1:
        paired = [terms[i] + terms[i + 1] for i in range(0, len(terms) - 1, 2)]
        terms = paired + ([terms[-1]] if len(terms) % 2 else [])
    return terms[0]


class Block:
    def __init__(self, p):
        self.n = len(p)
        if self.n == 2:
            a, b, c = p[0][0], p[1][0], p[1][1]
            det = a * c - b * b
            q = 1.0 / det
            self.entries = (a, b, det)
            self.inverse = (c * q, -b * q, a * q)
            return
        h = self.n // 2
        self.first = Block([row[:h] for row in p[:h]])
        below = [[p[h + x][y] for y in range(h)] for x in range(h)]
        self.gain = [self.first.solve(row) for row in below]
        self.second = Block(
            [
                [p[h + x][h + y] - sum_products(self.gain[x], below[y]) for y in range(x + 1)]
                for x in range(h)
            ]
        )

    def reduce(self, rows):
        h = self.n // 2
        return [rows[h + x] - sum_products(self.gain[x], rows[:h]) for x in range(h)]

    def solve(self, rows):
        if self.n == 2:
            i00, i01, i11 = self.inverse
            return [i00 * rows[0] + i01 * rows[1], i01 * rows[0] + i11 * rows[1]]
        h = self.n // 2
        top = self.first.solve(rows[:h])
        bottom = self.second.solve(self.reduce(rows))
        top = [
            top[y] - sum_products([self.gain[x][y] for x in range(h)], bottom) for y in range(h)
        ]
        return top + bottom

    def half_solve(self, rows):
        if self.n == 2:
            a, b, det = self.entries
            scale = lax.rsqrt(a)
            inv_a = scale * scale
            return [
                rows[0] * scale,
                (rows[1] - (b * inv_a) * rows[0]) * lax.rsqrt(det * inv_a),
            ]
        return self.first.half_solve(rows[: self.n // 2]) + self.second.half_solve(
            self.reduce(rows)
        )


def factor_diagonal(tiles):
    tiles = list(tiles)
    lanes = lax.broadcasted_iota(jnp.int32, (8, 128), 1)
    subs = lax.broadcasted_iota(jnp.int32, (8, 128), 0)
    upper, inverse = [], []
    for v in range(16):
        j = 8 * v
        inside = (lanes >= j) & (lanes < j + SUBS)
        cols = [
            {i: jnp.broadcast_to(tiles[i][:, j + k : j + k + 1], (8, 128)) for i in range(v, 16)}
            for k in range(SUBS)
        ]
        rows = [jnp.broadcast_to(tiles[v][k : k + 1, :], (8, 128)) for k in range(SUBS)]
        pivots = [
            [jnp.broadcast_to(cols[l][v][k : k + 1, :], (8, 128)) for l in range(k + 1)]
            for k in range(SUBS)
        ]
        unit_rows = [
            jnp.where(inside, jnp.where(lanes == j + k, F32(1), F32(0)), rows[k])
            for k in range(SUBS)
        ]
        block = Block(pivots)
        solved = block.solve(unit_rows)
        up, inv = block.half_solve(rows), block.half_solve(unit_rows)
        up_tile, inv_tile = up[0], inv[0]
        for k in range(1, SUBS):
            up_tile = jnp.where(subs == k, up[k], up_tile)
            inv_tile = jnp.where(subs == k, inv[k], inv_tile)
        upper.append(jnp.where(lanes >= subs + j, up_tile, F32(0)))
        inverse.append(jnp.where(lanes <= subs + j, inv_tile, F32(0)))
        for i in range(v + 1, 16):
            tiles[i] = jnp.where(inside, F32(0), tiles[i]) - sum_products(
                [cols[k][i] for k in range(SUBS)], solved
            )
    return upper, inverse


AXES = ("x", "y", "z")
CUTS = ((0, 384), (384, 384), (768, 256))
ORDERS = (("y", "z", "x"), ("z", "x", "y"), ("x", "y", "z"))
LINKS = 128


class Mover:
    def __init__(self, send_sems, recv_sems):
        self.send_sems, self.recv_sems = send_sems, recv_sems
        row, col, grp = lax.axis_index("row"), lax.axis_index("col"), lax.axis_index("grp")
        self.row = row
        self.core = lax.rem(row, 2)
        self.at = {"x": row // 2, "y": grp * 2 + col // 4, "z": lax.rem(col, 4)}
        self.count = 0
        self.sent = []

    def device(self, axis, place):
        if axis == "x":
            return {"row": place * 2 + self.core}
        if axis == "y":
            return {"grp": place // 2, "col": lax.rem(place, 2) * 4 + self.at["z"]}
        return {"col": (self.at["y"] - self.at["y"] // 2 * 2) * 4 + place}

    def sibling(self):
        return {"row": self.row + 1 - 2 * self.core}

    def shifted(self, axis, by):
        return lax.rem(self.at[axis] + (by + 4), 4)

    def greet(self):
        barrier = pltpu.get_barrier_semaphore()
        others = [self.sibling()]
        for axis in AXES:
            others += [self.device(axis, self.shifted(axis, by)) for by in (1, 2, 3)]
        for other in others:
            pl.semaphore_signal(
                barrier, inc=1, device_id=other, device_id_type=pl.DeviceIdType.MESH
            )
        pl.semaphore_wait(barrier, len(others))

    def make(self, src, dst, device, send=True):
        i = self.count
        self.count += 1
        copy = pltpu.make_async_remote_copy(
            src_ref=src,
            dst_ref=dst,
            send_sem=self.send_sems.at[i],
            recv_sem=self.recv_sems.at[i],
            device_id=device,
            device_id_type=pl.DeviceIdType.MESH,
        )
        return copy

    def ring(self, axis, region, when=None):
        here = self.at[axis]
        ahead, behind = self.shifted(axis, 1), self.shifted(axis, -1)
        toward = lax.rem(here + 1 + 2 * self.core, 4)
        away = lax.rem(here + 3 - 2 * self.core, 4)
        plus = self.make(region(here), region(here), self.device(axis, ahead))
        minus = self.make(region(here), region(here), self.device(axis, behind))
        passed = self.make(region(away), region(away), self.device(axis, toward))
        self.sent += [(c, when) for c in (plus, minus, passed)]

        def first():
            plus.start()
            minus.start()

        def second():
            plus.wait_recv()
            minus.wait_recv()
            passed.start()

        def third():
            passed.wait_recv()

        return [guard(when, f) for f in (first, second, third)]

    def scatter(self, axis, source, target, when=None):
        here = self.at[axis]
        root, leaf = here == 0, here != 0
        if when is not None:
            root, leaf = root & when, leaf & when
        i = self.count
        self.count += 3
        recv = self.recv_sems.at[i]
        copies = []
        for k in (1, 2, 3):
            copies.append(
                pltpu.make_async_remote_copy(
                    src_ref=source(k),
                    dst_ref=target(k),
                    send_sem=self.send_sems.at[i + k - 1],
                    recv_sem=recv,
                    device_id=self.device(axis, k),
                    device_id_type=pl.DeviceIdType.MESH,
                )
            )
        self.sent += [(c, root) for c in copies]

        def first():
            for c in copies:
                c.start()

        def second():
            copies[0].wait_recv()

        return [guard(root, first), guard(leaf, second)]

    def push(self, region, when=None, taken=None):
        copy = self.make(region, region, self.sibling())
        self.sent.append((copy, when))
        return guard(when, copy.start), guard(taken, copy.wait_recv)

    def finish(self):
        for copy, when in self.sent:
            guard(when, copy.wait_send)()


def guard(when, f):
    if when is None:
        return f

    def guarded():
        pl.when(when)(f)

    return guarded


def merge(*steps):
    def run():
        for s in steps:
            s()

    return run


def rows_of(ref, start, count, cols=None):
    start = pl.multiple_of(start, 16)
    if cols is None:
        return ref.at[pl.ds(start, count)]
    return ref.at[pl.ds(start, count), pl.ds(*cols)]


def gather_program(
    raw, parent, g_ref, d_ref, st_ref, m_ref, u_ref, e_ref, lead, m_far, e_x, e_y, st_a, sems
):
    send_sems, recv_sems, local_sems = sems
    mv = Mover(send_sems, recv_sems)
    x, y, z, core = mv.at["x"], mv.at["y"], mv.at["z"], mv.core
    locals_made = []

    def local(src, dst, when=None):
        copy = pltpu.make_async_copy(src, dst, local_sems.at[len(locals_made)])
        locals_made.append(copy)
        return guard(when, copy.start), guard(when, copy.wait)

    def block(place, cut):
        gy = (place["y"] // 2, lax.rem(place["y"], 2)) if "y" in place else (slice(None),) * 2
        px = place.get("x", slice(None))
        pz = place.get("z", slice(None))
        return g_ref.at[gy[0], px, core, gy[1], pz, :, pl.ds(*cut)]

    own = local(raw, g_ref.at[y // 2, x, core, lax.rem(y, 2), z])
    a_lists = []
    for cut, order in zip(CUTS, ORDERS):
        place = dict(mv.at)
        steps = []
        for stage, axis in enumerate(order):
            ring = mv.ring(axis, lambda k, p=dict(place), a=axis: block({**p, a: k}, cut))
            if stage == 2:
                base = mv.push(block(place, cut))
                near = [mv.push(block({**place, axis: mv.shifted(axis, by)}, cut)) for by in (1, 3)]
                far = mv.push(block({**place, axis: mv.shifted(axis, 2)}, cut))
                ring[0] = merge(ring[0], base[0])
                ring[1] = merge(ring[1], near[0][0], near[1][0])
                ring[2] = merge(ring[2], far[0])
                ring.append(merge(base[1], near[0][1], near[1][1], far[1]))
            steps += ring
            del place[axis]
        a_lists.append(steps)

    lead_core = core == 0
    part_d = lambda k: rows_of(d_ref, k * 256, 256)
    d_root = local(parent.at[pl.ds(0, 256)], d_ref.at[pl.ds(0, 256)], lead_core & (x == 0))
    hand = mv.scatter("x", lambda k: rows_of(parent, k * 256, 256), part_d, lead_core)
    turn = mv.ring("x", part_d, lead_core)
    push = mv.push(d_ref, lead_core, core == 1)
    d_steps = [
        merge(d_root[0], hand[0]),
        merge(d_root[1], hand[1], turn[0]),
        turn[1],
        merge(turn[2], push[0]),
        push[1],
    ]

    e_row = x * 256 + y * 64 + z * 16
    cut_z = lambda k: rows_of(e_ref, x * 256 + y * 64 + k * 16, 16)
    cut_y = lambda k: rows_of(e_ref, x * 256 + k * 64, 64)
    cut_x = lambda k: rows_of(e_ref, k * 256, 256)
    on_x = lead_core & (y == 0) & (z == 0)
    on_y = lead_core & (z == 0)
    loc_x = local(parent.at[pl.ds(0, 256)], e_x, on_x & (x == 0))
    loc_y = local(e_x.at[pl.ds(0, 64)], e_y, on_y & (y == 0))
    loc_z = local(e_y.at[pl.ds(0, 16)], rows_of(e_ref, e_row, 16), on_y)
    hand_x = mv.scatter("x", lambda k: rows_of(parent, k * 256, 256), lambda k: e_x, on_x)
    hand_y = mv.scatter("y", lambda k: e_x.at[pl.ds(64 * k, 64)], lambda k: e_y, on_y)
    hand_z = mv.scatter("z", lambda k: e_y.at[pl.ds(16 * k, 16)], cut_z, lead_core)
    turn_z = mv.ring("z", cut_z, lead_core)
    turn_y = mv.ring("y", cut_y, lead_core)
    turn_x = mv.ring("x", cut_x, lead_core)
    push = mv.push(e_ref, lead_core, core == 1)
    e_steps = [
        merge(loc_x[0], hand_x[0]),
        merge(loc_x[1], hand_x[1], loc_y[0], hand_y[0]),
        merge(loc_y[1], hand_y[1], loc_z[0], hand_z[0]),
        merge(loc_z[1], hand_z[1], turn_z[0]),
        turn_z[1],
        merge(turn_z[2], turn_y[0]),
        turn_y[1],
        merge(turn_y[2], turn_x[0]),
        turn_x[1],
        merge(turn_x[2], push[0]),
        push[1],
    ]

    st_lists = []
    for i, ((a, b), cut) in enumerate(((("z", "y"), (0, 512)), (("y", "z"), (512, 512)))):
        wide = lambda k, cut=cut: rows_of(st_ref, k * 512, 512, cut)
        wide_source = lambda k, cut=cut: rows_of(parent, k * 512, 512, cut)
        fine = lambda k, a=a, cut=cut: rows_of(st_ref, mv.at[a] * 512 + k * 128, 128, cut)
        held = st_a.at[i]
        line = mv.at[b] == 0
        loc_a = local(wide_source(0), held, line & (mv.at[a] == 0))
        loc_b = local(held.at[pl.ds(0, 128)], fine(0), line)
        hand_a = mv.scatter(a, wide_source, lambda k: held, line)
        hand_b = mv.scatter(b, lambda k: held.at[pl.ds(k * 128, 128)], fine)
        turn_b = mv.ring(b, fine)
        turn_a = mv.ring(a, wide)
        st_lists.append(
            [
                merge(loc_a[0], hand_a[0]),
                merge(loc_a[1], hand_a[1], loc_b[0], hand_b[0]),
                merge(loc_b[1], hand_b[1], turn_b[0]),
                turn_b[1],
                merge(turn_b[2], turn_a[0]),
                turn_a[1],
                turn_a[2],
            ]
        )

    y_lo = lax.rem(y, 2)
    base = core * (2 * 4 * raw.shape[0])
    size = raw.shape[0]
    chunk_z = lambda k: rows_of(u_ref, base + (y_lo * 4 + k) * size, size)
    u_own = local(raw, chunk_z(z), x == 0)
    u_hand = mv.scatter("x", lambda k: raw, lambda k: chunk_z(z))
    u_turn = mv.ring("z", chunk_z)
    full = 8 * size
    rest = e_ref.shape[0] - full
    beside = {"col": (1 - y_lo) * 4 + z}
    half = rows_of(u_ref, y_lo * 4 * size, 4 * size)
    swap = mv.make(half, half, beside)
    mv.sent.append((swap, lead_core))
    tail = u_ref.at[pl.ds(full, rest)]
    slide = mv.make(tail, tail, beside)
    mv.sent.append((slide, (core == 1) & (y_lo == 0)))
    push_head = mv.push(u_ref.at[pl.ds(0, full)], lead_core, core == 1)
    push_tail = mv.push(tail, core == 1, lead_core)
    u_steps = [
        merge(u_own[0], u_hand[0]),
        merge(u_own[1], u_hand[1], u_turn[0]),
        u_turn[1],
        merge(
            u_turn[2],
            guard(lead_core, swap.start),
            guard((core == 1) & (y_lo == 0), slide.start),
        ),
        merge(
            guard(lead_core, swap.wait_recv),
            guard((core == 1) & (y_lo == 1), slide.wait_recv),
            push_head[0],
            push_tail[0],
        ),
        merge(push_head[1], push_tail[1]),
    ]

    def exchange(mine, theirs):
        start = core * 512 + x * 128 + z * 32
        across = mv.make(mine(start, 32), theirs(start, 32), mv.device("y", mv.shifted("y", 2)))
        mv.sent.append((across, None))
        turn_z = mv.ring("z", lambda k: theirs(core * 512 + x * 128 + k * 32, 32))
        turn_x = mv.ring("x", lambda k: theirs(core * 512 + k * 128, 128))
        push = mv.push(theirs(core * 512, 512))
        return [
            across.start,
            merge(across.wait_recv, turn_z[0]),
            turn_z[1],
            merge(turn_z[2], turn_x[0]),
            turn_x[1],
            merge(turn_x[2], push[0]),
            push[1],
        ]

    def part(ref, *lead_index):
        return lambda start, n: ref.at[lead_index + (pl.ds(pl.multiple_of(start, 16), n),)]

    x_steps = exchange(part(lead, 0), part(lead, 1))
    m_steps = exchange(part(m_ref, slice(None)), part(m_far, slice(None)))
    assert mv.count <= LINKS
    a, st = [[merge(*s) for s in zip(*lists)] for lists in (a_lists, st_lists)]
    d, e, u, m = d_steps, e_steps, u_steps, m_steps
    early = [
        merge(mv.greet, own[0], u[0], e[0], own[1], a[0]),
        merge(u[1], e[1]),
        a[1],
        merge(u[2], e[2]),
        merge(u[3], a[2], a[3]),
        e[3],
        merge(u[4], e[4]),
        e[5],
        merge(a[4], e[6]),
        merge(e[7], d[0]),
        merge(u[5], e[8]),
        merge(a[5], a[6], e[9]),
        merge(e[10], d[1]),
        d[2],
        st[0],
    ]
    late = [
        merge(m[0], d[3]),
        a[7],
        merge(m[1], st[1]),
        d[4],
        merge(m[2], st[2]),
        a[8],
        merge(m[3], st[3]),
        m[4],
        st[4],
        m[5],
        st[5],
        m[6],
        merge(st[6], a[9]),
    ]
    return mv, early, x_steps, late


def factor_loop(w, inv_s, up_s, l_ref, ticks):
    width = w.shape[0]
    steps = width // NB
    if l_ref is not None:
        l_ref[...] = jnp.zeros_like(l_ref)

    def step(k, _):
        o = pl.multiple_of(k * NB, NB)
        here = pl.ds(o, NB)
        for i in range(0, len(ticks), 2):
            pl.when(k == i // 2)(ticks[i])
        groups = [w[pl.ds(pl.multiple_of(o + 8 * i, 8), 8), here] for i in range(NB // 8)]
        up, inv = factor_diagonal(groups)
        for i in range(NB // 8):
            inv_s[8 * i : 8 * i + 8, :] = inv[i]
            up_s[8 * i : 8 * i + 8, :] = up[i]
        inverse = inv_s[...]
        w[:, here] = dot_nt(w[:, here], inverse)
        w[here, here] = inverse.T
        if l_ref is not None:
            l_ref[here, here] = up_s[...].T

            def keep(j, _):
                below = pl.ds(pl.multiple_of(j * NB, NB), NB)
                l_ref[below, here] = w[below, here]
                return 0

            lax.fori_loop(k + 1, steps, keep, 0)
        for i in range(1, len(ticks), 2):
            pl.when(k == i // 2)(ticks[i])

        def update(j, _):
            there = pl.ds(pl.multiple_of(j * NB, NB), NB)
            w[here, there] = jnp.zeros((NB, NB), F32)
            w[:, there] -= dot_nt(w[:, here], w[there, here])
            return 0

        lax.fori_loop(k + 1, steps, update, 0)
        return 0

    lax.fori_loop(0, steps, step, 0)


def split_upper(w, m_ref):
    width = w.shape[0]
    for n in range(width // NB):
        cut = slice(n * NB, (n + 1) * NB)
        end = (n + 1) * NB
        hi, lo = split(w[:end, cut])
        m_ref[0, :end, cut] = hi
        m_ref[1, :end, cut] = lo
        if end < width:
            m_ref[:, end:, cut] = jnp.zeros((2, width - end, NB), BF16)


def front_kernel(
    a_ref, keep_ref, raw, parent,
    m_ref, m_pivot, l_ref, g_ref, d_ref, st_ref, lead_out, far_out,
    w, inv_s, up_s, u_ref, e_ref, lead, m_far, e_x, e_y, st_a, send_sems, recv_sems, local_sems,
):
    width = a_ref.shape[0]
    mv, early, swap, late = gather_program(
        raw, parent, g_ref, d_ref, st_ref, m_ref, u_ref, e_ref, lead, m_far, e_x, e_y, st_a,
        (send_sems, recv_sems, local_sems),
    )
    w[...] = a_ref[...]
    factor_loop(w, inv_s, up_s, None, early)
    split_upper(w, m_ref)
    for n in range(width // CUT):
        end = (n + 1) * CUT
        cut = slice(n * CUT, end)
        rows = u_ref[:width, :end]
        both = dot16(rows, m_ref[0, :end, cut]) + dot16(rows, m_ref[1, :end, cut])
        lead[0, :, cut] = (both * keep_ref[:, :1]).astype(BF16)
    for step in swap:
        step()
    lead_copy = pltpu.make_async_copy(lead, lead_out, local_sems.at[14])
    far_copy = pltpu.make_async_copy(m_far, far_out, local_sems.at[15])
    lead_copy.start()
    for n in range(width // CUT):
        start = n * CUT
        cut = slice(start, start + CUT)
        total = e_ref[start:, cut].astype(F32)
        for i in range(2):
            total -= dot16(lead[i, start:, :], lead[i, cut, :], NT)
        w[start:, cut] = total
    factor_loop(w, inv_s, up_s, l_ref, late)
    far_copy.start()
    split_upper(w, m_pivot)
    mv.finish()
    lead_copy.wait()
    far_copy.wait()


def front(block, keep, raw, parent):
    width = block.shape[0]
    chunk = raw.shape[0]
    hbm = pl.BlockSpec(memory_space=pl.ANY)
    vmem = pl.BlockSpec(memory_space=VM)
    pair = jax.ShapeDtypeStruct((2, width, width), BF16)
    return pl.pallas_call(
        front_kernel,
        out_shape=[
            pair,
            pair,
            jax.ShapeDtypeStruct((width, width), F32),
            jax.ShapeDtypeStruct((2, 4, 2, 2, 4, chunk, width), BF16),
            jax.ShapeDtypeStruct((width, width), BF16),
            jax.ShapeDtypeStruct(parent.shape, BF16),
            pair,
            pair,
        ],
        in_specs=[vmem, vmem, hbm, hbm],
        out_specs=[vmem, vmem, vmem, hbm, hbm, hbm, hbm, hbm],
        scratch_shapes=[
            VM((width, width), F32),
            VM((NB, NB), F32),
            VM((NB, NB), F32),
            VM((16 * chunk, width), BF16),
            VM((width, width), BF16),
            VM((2, width, width), BF16),
            VM((2, width, width), BF16),
            VM((256, width), BF16),
            VM((64, width), BF16),
            VM((2, 512, 512), BF16),
            pltpu.SemaphoreType.DMA((LINKS,)),
            pltpu.SemaphoreType.DMA((LINKS,)),
            pltpu.SemaphoreType.DMA((16,)),
        ],
        compiler_params=pltpu.CompilerParams(
            vmem_limit_bytes=52 * 2**20, collective_id=0, has_side_effects=True
        ),
        cost_estimate=pl.CostEstimate(
            flops=120_000_000_000, bytes_accessed=16 * width * width, transcendentals=0
        ),
        name="front",
    )(block, keep, raw, parent)


def chunk_span(chunk):
    return -(-(TB + chunk - 16) // chunk)


def spread_kernel(
    chunk, tile_ref, have_ref, grp_ref, gathered, own_ref, far_ref, lead_ref, d_ref, st_ref,
    s_ref, b_ref, buf, sem,
):
    t, g = pl.program_id(0), pl.program_id(1)
    width = lead_ref.shape[1]
    chunks = gathered.shape[1]
    across = 2
    span = chunk_span(chunk)
    slot = lax.rem(t * 2 + g, 2)

    def copies(t, g, slot):
        row = tile_ref[g * 6 + t] * TB
        first = row // chunk
        out = []
        for i in range(span):
            c = jnp.minimum(first + i, chunks - 1)
            out.append(
                pltpu.make_async_copy(
                    gathered.at[g ^ grp_ref[0], c],
                    buf.at[slot, pl.ds(i * chunk, chunk)],
                    sem.at[slot, i],
                )
            )
        return out

    @pl.when((t == 0) & (g == 0))
    def _():
        for c in copies(t, g, slot):
            c.start()

    nxt = t * 2 + g + 1

    @pl.when(nxt < 12)
    def _():
        for c in copies(nxt // 2, lax.rem(nxt, 2), 1 - slot):
            c.start()

    for c in copies(t, g, slot):
        c.wait()

    @pl.when((g == 0) & (t < across))
    def _():
        b_ref[...] = d_ref[...].astype(F32).T

    @pl.when((g == 0) & (t >= across))
    def _():
        b_ref[...] = st_ref[...].astype(F32)

    have = have_ref[g * 6 + t] != 0

    @pl.when(jnp.logical_not(have))
    def _():
        s_ref[...] = jnp.zeros_like(s_ref)

    row = tile_ref[g * 6 + t] * TB
    rows = pl.ds(pl.multiple_of(lax.rem(row, chunk), 16), TB)

    def fill(m_ref):
        for n in range(width // CUT):
            end = (n + 1) * CUT
            cut = slice(n * CUT, end)
            held = buf[slot, rows, :end]
            part = dot16(held, m_ref[0, :end, cut]) + dot16(held, m_ref[1, :end, cut])
            s_ref[:, cut] = part.astype(BF16)
        b_ref[...] -= dot16(s_ref[...], lead_ref[g], NT)

    pl.when(have & (g == 0))(lambda: fill(own_ref))
    pl.when(have & (g == 1))(lambda: fill(far_ref))


def spread(tiles, have, grp, gathered, m_own, m_far, lead_both, column_panel, stripe):
    chunk = gathered.shape[2]
    width = lead_both.shape[-1]
    across = column_panel.shape[1] // TB
    rows = column_panel.shape[1] + stripe.shape[0]
    vmem = pl.BlockSpec(memory_space=VM)
    return pl.pallas_call(
        functools.partial(spread_kernel, chunk),
        grid_spec=pltpu.PrefetchScalarGridSpec(
            num_scalar_prefetch=3,
            grid=(rows // TB, 2),
            in_specs=[
                pl.BlockSpec(memory_space=pl.ANY),
                vmem,
                vmem,
                vmem,
                pl.BlockSpec((width, TB), lambda t, g, *_: (0, jnp.minimum(t, across - 1))),
                pl.BlockSpec((TB, width), lambda t, g, *_: (jnp.maximum(t - across, 0), 0)),
            ],
            out_specs=[
                pl.BlockSpec((TB, width), lambda t, g, *_: (t, g)),
                pl.BlockSpec((TB, width), lambda t, g, *_: (t, 0)),
            ],
            scratch_shapes=[
                VM((2, chunk_span(chunk) * chunk, width), BF16),
                pltpu.SemaphoreType.DMA((2, chunk_span(chunk))),
            ],
        ),
        out_shape=[
            jax.ShapeDtypeStruct((rows, 2 * width), BF16),
            jax.ShapeDtypeStruct((rows, width), F32),
        ],
        compiler_params=pltpu.CompilerParams(vmem_limit_bytes=52 * 2**20),
        cost_estimate=pl.CostEstimate(
            flops=35_000_000_000, bytes_accessed=40 * 2**20, transcendentals=0
        ),
        name="spread",
    )(tiles, have, grp, gathered, m_own, m_far, lead_both, column_panel, stripe)


def trailing_kernel(across, flag_ref, s_ref, b_ref, m_ref, l_ref, parent_ref, out_ref, s_keep, f_keep):
    t = pl.program_id(0)
    width = b_ref.shape[1]
    b_hi, b_lo = split(b_ref[...])
    panels = []
    for n in range(width // CUT):
        end = (n + 1) * CUT
        cut = slice(n * CUT, end)
        hi, lo = m_ref[0, :end, cut], m_ref[1, :end, cut]
        panels.append(
            dot16(b_hi[:, :end], hi) + dot16(b_hi[:, :end], lo) + dot16(b_lo[:, :end], hi)
        )

    @pl.when(t < across)
    def _():
        here = pl.ds(pl.multiple_of(t * TB, TB), TB)
        s_keep[here, :] = s_ref[...]
        for n in range(width // CUT):
            f_keep[here, n * CUT : (n + 1) * CUT] = panels[n].astype(BF16)

    @pl.when(t >= across)
    def _():
        first = flag_ref[0] != 0
        pivot = (flag_ref[1] != 0) & (t < across + width // TB)

        @pl.when(first & pivot)
        def _():
            out_ref[...] = l_ref[...]

        @pl.when(first & jnp.logical_not(pivot))
        def _():
            for n in range(width // CUT):
                out_ref[:, n * CUT : (n + 1) * CUT] = panels[n]

        @pl.when(jnp.logical_not(first) & pivot)
        def _():
            out_ref[...] = jnp.zeros_like(out_ref)

        @pl.when(jnp.logical_not(first) & jnp.logical_not(pivot))
        def _():
            f = jnp.concatenate([p.astype(BF16) for p in panels], axis=1)
            out_ref[...] = parent_ref[...].astype(F32) - (
                dot16(s_ref[...], s_keep[...], NT) + dot16(f, f_keep[...], NT)
            )


def trailing(flags, s_all, b_all, m_pivot, pivot_factor, parent):
    width = b_all.shape[1]
    cols = parent.shape[1]
    across = cols // TB
    tiles = parent.shape[0] // TB
    lead = width // TB
    return pl.pallas_call(
        functools.partial(trailing_kernel, across),
        grid_spec=pltpu.PrefetchScalarGridSpec(
            num_scalar_prefetch=1,
            grid=(across + tiles,),
            in_specs=[
                pl.BlockSpec((TB, 2 * width), lambda t, *_: (t, 0)),
                pl.BlockSpec((TB, width), lambda t, *_: (t, 0)),
                pl.BlockSpec(memory_space=VM),
                pl.BlockSpec((TB, width), lambda t, *_: (jnp.clip(t - across, 0, lead - 1), 0)),
                pl.BlockSpec((TB, cols), lambda t, *_: (jnp.maximum(t - across, 0), 0)),
            ],
            out_specs=pl.BlockSpec((TB, cols), lambda t, *_: (jnp.maximum(t - across, 0), 0)),
            scratch_shapes=[VM((cols, 2 * width), BF16), VM((cols, width), BF16)],
        ),
        out_shape=jax.ShapeDtypeStruct(parent.shape, F32),
        compiler_params=pltpu.CompilerParams(vmem_limit_bytes=56 * 2**20),
        cost_estimate=pl.CostEstimate(flops=35_000_000_000, bytes_accessed=40 * 2**20, transcendentals=0),
        name="trailing",
    )(flags, s_all, b_all, m_pivot, pivot_factor, parent)


def locate(tile_map, parent_tiles):
    matches = tile_map[:, None] == jnp.arange(parent_tiles, dtype=jnp.int32)[None, :]
    positions = jnp.arange(tile_map.shape[0], dtype=jnp.int32)[:, None]
    return jnp.sum(jnp.where(matches, positions, 0), axis=0), jnp.any(matches, axis=0)


def per_device(child_update, child_pivot, child_map, parent_front):
    width = child_pivot.shape[-1]
    stripe_rows, block_cols = parent_front.shape
    row_tiles = stripe_rows // TB
    col_tiles = block_cols // TB
    parent_tiles = row_tiles * lax.axis_size("row")
    row = lax.axis_index("row")
    block = lax.axis_index(("grp", "col"))
    raw = child_update[0]
    chunk = raw.shape[0]

    grp = lax.axis_index("grp")
    own_map = jnp.where(grp == 0, child_map, child_map[::-1])
    lead_tiles = jnp.arange(width // TB, dtype=jnp.int32)
    keep = (own_map[0, : width // TB] == lead_tiles).astype(F32)
    keep = jnp.broadcast_to(jnp.repeat(keep, TB)[:, None], (width, 128))
    m_own, m_pivot, pivot_factor, gathered, column_panel, stripe, lead_both, m_far = front(
        child_pivot[0], keep, raw, parent_front
    )
    gathered = gathered.reshape(2, -1, chunk, width)

    wanted_tiles = jnp.concatenate(
        [
            block * col_tiles + jnp.arange(col_tiles, dtype=jnp.int32),
            row * row_tiles + jnp.arange(row_tiles, dtype=jnp.int32),
        ]
    )
    tiles, have = [], []
    for g in range(2):
        inverse, present = locate(own_map[g], parent_tiles)
        tiles.append(inverse[wanted_tiles])
        have.append(present[wanted_tiles].astype(jnp.int32))
    tiles, have = jnp.concatenate(tiles), jnp.concatenate(have)
    s_all, b_all = spread(
        tiles, have, grp[None], gathered, m_own, m_far, lead_both, column_panel, stripe
    )
    flags = jnp.stack([block == 0, row == 0]).astype(jnp.int32)
    return trailing(flags, s_all, b_all, m_pivot, pivot_factor, parent_front)


def solution(mesh):
    in_specs = (P("grp", ("row", "col"), None), P("grp", None, None), P(), P("row", ("grp", "col")))
    out_specs = P("row", ("grp", "col"))
    return jax.shard_map(
        per_device, mesh=mesh, in_specs=in_specs, out_specs=out_specs, check_vma=False
    )
```

time: 1310 us -> 343 us (0.26)
  other arithmetic: 544 us -> 1.09 us
  waiting for transfers between devices: 383 us -> 0 us
  Pallas kernels: 0 us -> 333 us
  matrix products: 180 us -> 0 us
  local copies, waits for them, and re-layouts: 168 us -> 4.51 us
  between operations: 26.3 us -> 0.05 us
    another operation x70 -> x0, other arithmetic: 507 us -> none  [the longest x29 171 us: factor_pair(): first_factor = jnp.linalg.cholesky(block[:half, :half])]
    all_gather x1 -> x0, waiting for transfers between devices: 383 us -> none  [per_device(): lax.all_gather(local_panel[None], ('grp', 'row', 'col'), axis=1, tiled=True)]
    pallas_call x0 -> x3, Pallas kernels: none -> 333 us  [the longest x1 251 us: front(): pl.pallas_call(front_kernel, out_shape=[pair, pair, jax.ShapeDtypeStruct(...]
    dot_general x15 -> x0, matrix products: 125 us -> none  [the longest x4 49.9 us: outer_sum(): lax.dot_general(left_rows, right_rows, (((1,), (1,)), ((), ())), preferre...]
    another operation x52 -> x0, matrix products: 55.6 us -> none  [the longest x14 18.6 us: factor_pair(): lax.linalg.triangular_solve(second_factor, identity, left_side=True, lowe...]
    another operation x72 -> x0, local copies, waits for them, and re-layouts: 50.9 us -> none  [the longest x24 27.6 us: factor_pair(): lax.linalg.triangular_solve(second_factor, identity, left_side=True, lowe...]
    gather x6 -> x4, local copies, waits for them, and re-layouts: 42.1 us -> 2.59 us  [the longest x2 1.3 us: per_device(): tiles.append(inverse[wanted_tiles])]
    select_n x8 -> x2, other arithmetic: 26.7 us -> 0.08 us  [the longest x1 0.08 us: per_device(): tiles.append(inverse[wanted_tiles])]
  transfers between devices with their start and end apart: 3 -> 0, of which waited for: 1 -> 0; matrix products, arithmetic and copies ran while one was open for 30% -> 0% of each run, Pallas kernels for 0% -> 0%
where the time goes in v1:
time: 343 us; the launch traced here: 339 us
  Pallas kernels  333 us (97%)
  local copies, waits for them, and re-layouts  4.51 us (1%)
    pallas_call x1, Pallas kernels, front(): pl.pallas_call(front_kernel, out_shape=[pair, pair, jax.ShapeDtypeStruct(...  251 us
    pallas_call x1, Pallas kernels, spread(): pl.pallas_call(functools.partial(spread_kernel, chunk), grid_spec=pltpu.P...  46.3 us
    pallas_call x1, Pallas kernels, trailing(): pl.pallas_call(functools.partial(trailing_kernel, across), grid_spec=pltp...  35.7 us

profile of v1, /device:TPU:49, one launch (start us, length us, event | category | flops | bytes accessed | tf_op | source)
XLA Modules:
  0.0 338.8 jit_solution(11413671378961509712)
XLA Ops:
  0.0 0.7 add_convert_fusion.flag_ref
  0.7 0.1 fusion.2
  0.7 0.7 rev.3
  1.5 0.1 fusion
  1.6 0.1 select_reduce_fusion
  1.7 0.6 gather_fusion.3
  2.3 0.7 gather_fusion.2
  3.0 0.1 add_convert_fusion.1.have_ref
  3.0 0.6 gather_fusion.1
  3.7 0.6 gather_fusion
  4.3 0.1 pad_add_fusion.tile_ref
  4.4 0.1 broadcast_bitcast_fusion
  4.5 0.2 broadcast_in_dim.45.keep_ref
  4.7 0.0 copy-start
  4.7 0.9 copy-done
  5.6 251.2 %front.1 = (bf16[2,1024,1024]{2,1,0:T(8,128)(2,1)}, bf16[2,1024,1024]{2,1,0:T(8,128)(2,1)}, f32[1024,1024]{1,0:T(8,128)}, bf16[2,4,2,2,4,112,1024]{6,5,4,3,2,1,0...) custom-call(f32[1024,1024]{1,0:T(8,128)} %bitcast.23, ...), custom_call_target="tpu_custom_call" | custom-call | flops 120000004096 | bytes 16777216 | tf_op jit(solution)/shard_map/front/pallas_call | solution.py:580
  256.9 46.3 %spread.1 = (bf16[3072,2048]{1,0:T(8,128)(2,1)}, f32[3072,1024]{1,0:T(8,128)}) custom-call(s32[12]{0:T(128)S(1)} %pad_add_fusion.tile_ref, s32[12]{0:T(128)S(1)} %add_convert_fusion.1.have_ref, s32[1]{0:T(128)} %bitcast.7.grp_ref, bf16[2,64,112,1024]{3,2,1,0:T(8,128)(2,1)} %bitcast.24, bf16[2,1024,1024]{2,1,0:T(8,128)(2,1)} %get-tuple-element.16.own_ref, ...), custom_call_target="tpu_custom_call" | custom-call | flops 35000000512 | bytes 41943040 | tf_op jit(solution)/shard_map/spread/pallas_call | solution.py:700
  303.2 35.7 %trailing.1 = f32[2048,1024]{1,0:T(8,128)} custom-call(s32[2]{0:T(128)} %add_convert_fusion.flag_ref, bf16[3072,2048]{1,0:T(8,128)(2,1)} %get-tuple-element.21.s_ref, f32[3072,1024]{1,0:T(8,128)} %get-tuple-element.22.b_ref, bf16[2,1024,1024]{2,1,0:T(8,128)(2,1)} %get-tuple-element.23.m_ref, f32[1024,1024]{1,0:T(8,128)} %get-tuple-element.24.l_ref, ...), custom_call_target="tpu_custom_call" | custom-call | flops 35000000512 | bytes 41943040 | tf_op jit(solution)/shard_map/trailing/pallas_call | solution.py:786
  (7 shorter events, 0.0 us)
Async XLA Ops:
  4.7 0.9 copy-start

commit v2 on v1

--- a/solution.py
+++ b/solution.py
@@ -18,6 +18,7 @@
 
 
 CUT = 256
+WIDE = 512
 
 
 def dot16(a, b, dims=NN):
@@ -29,9 +30,11 @@
     return hi, (x - hi.astype(F32)).astype(BF16)
 
 
-def dot_nt(a, b):
-    return lax.dot_general(
-        a, b, NT, precision=lax.Precision.HIGHEST, preferred_element_type=F32
+def dot3(a, b):
+    ah, al = split(a)
+    bh, bl = split(b)
+    return dot16(
+        jnp.concatenate([ah, ah, al], axis=1), jnp.concatenate([bh, bl, bh], axis=1), NT
     )
 
 
@@ -132,9 +135,9 @@
 
 
 AXES = ("x", "y", "z")
-CUTS = ((0, 384), (384, 384), (768, 256))
+CUTS = ((0, 384), (384, 256), (640, 384))
 ORDERS = (("y", "z", "x"), ("z", "x", "y"), ("x", "y", "z"))
-LINKS = 128
+LINKS = 144
 
 
 class Mover:
@@ -275,7 +278,7 @@
 
 
 def gather_program(
-    raw, parent, g_ref, d_ref, st_ref, m_ref, u_ref, e_ref, lead, m_far, e_x, e_y, st_a, sems
+    raw, parent, g_ref, d_ref, st_ref, m_ref, u_ref, e_ref, lead, m_far, piece, e_y, e_z, st_a, sems
 ):
     send_sems, recv_sems, local_sems = sems
     mv = Mover(send_sems, recv_sems)
@@ -326,33 +329,33 @@
         push[1],
     ]
 
-    e_row = x * 256 + y * 64 + z * 16
-    cut_z = lambda k: rows_of(e_ref, x * 256 + y * 64 + k * 16, 16)
-    cut_y = lambda k: rows_of(e_ref, x * 256 + k * 64, 64)
-    cut_x = lambda k: rows_of(e_ref, k * 256, 256)
-    on_x = lead_core & (y == 0) & (z == 0)
-    on_y = lead_core & (z == 0)
-    loc_x = local(parent.at[pl.ds(0, 256)], e_x, on_x & (x == 0))
-    loc_y = local(e_x.at[pl.ds(0, 64)], e_y, on_y & (y == 0))
-    loc_z = local(e_y.at[pl.ds(0, 16)], rows_of(e_ref, e_row, 16), on_y)
-    hand_x = mv.scatter("x", lambda k: rows_of(parent, k * 256, 256), lambda k: e_x, on_x)
-    hand_y = mv.scatter("y", lambda k: e_x.at[pl.ds(64 * k, 64)], lambda k: e_y, on_y)
-    hand_z = mv.scatter("z", lambda k: e_y.at[pl.ds(16 * k, 16)], cut_z, lead_core)
+    e_row = y * 256 + z * 64 + x * 16
+    cut_x = lambda k: rows_of(e_ref, y * 256 + z * 64 + k * 16, 16)
+    cut_z = lambda k: rows_of(e_ref, y * 256 + k * 64, 64)
+    cut_y = lambda k: rows_of(e_ref, k * 256, 256)
+    on_y = lead_core & (x == 0) & (z == 0)
+    on_z = lead_core & (x == 0)
+    loc_y = local(parent.at[pl.ds(0, 256)], e_y, on_y & (y == 0))
+    loc_z = local(e_y.at[pl.ds(0, 64)], e_z, on_z & (z == 0))
+    loc_x = local(e_z.at[pl.ds(0, 16)], rows_of(e_ref, e_row, 16), on_z)
+    hand_y = mv.scatter("y", lambda k: rows_of(parent, k * 256, 256), lambda k: e_y, on_y)
+    hand_z = mv.scatter("z", lambda k: e_y.at[pl.ds(64 * k, 64)], lambda k: e_z, on_z)
+    hand_x = mv.scatter("x", lambda k: e_z.at[pl.ds(16 * k, 16)], cut_x, lead_core)
+    turn_x = mv.ring("x", cut_x, lead_core)
     turn_z = mv.ring("z", cut_z, lead_core)
     turn_y = mv.ring("y", cut_y, lead_core)
-    turn_x = mv.ring("x", cut_x, lead_core)
     push = mv.push(e_ref, lead_core, core == 1)
     e_steps = [
-        merge(loc_x[0], hand_x[0]),
-        merge(loc_x[1], hand_x[1], loc_y[0], hand_y[0]),
+        merge(loc_y[0], hand_y[0]),
         merge(loc_y[1], hand_y[1], loc_z[0], hand_z[0]),
-        merge(loc_z[1], hand_z[1], turn_z[0]),
+        merge(loc_z[1], hand_z[1], loc_x[0], hand_x[0]),
+        merge(loc_x[1], hand_x[1], turn_x[0]),
+        turn_x[1],
+        merge(turn_x[2], turn_z[0]),
         turn_z[1],
         merge(turn_z[2], turn_y[0]),
         turn_y[1],
-        merge(turn_y[2], turn_x[0]),
-        turn_x[1],
-        merge(turn_x[2], push[0]),
+        merge(turn_y[2], push[0]),
         push[1],
     ]
 
@@ -423,61 +426,68 @@
         mv.sent.append((across, None))
         turn_z = mv.ring("z", lambda k: theirs(core * 512 + x * 128 + k * 32, 32))
         turn_x = mv.ring("x", lambda k: theirs(core * 512 + k * 128, 128))
-        push = mv.push(theirs(core * 512, 512))
+        push = [
+            mv.push(theirs(core * 512 + mv.shifted("x", by) * 128, 128)) for by in (0, 1, 3, 2)
+        ]
         return [
             across.start,
             merge(across.wait_recv, turn_z[0]),
             turn_z[1],
-            merge(turn_z[2], turn_x[0]),
-            turn_x[1],
-            merge(turn_x[2], push[0]),
-            push[1],
+            merge(turn_z[2], turn_x[0], push[0][0]),
+            merge(turn_x[1], push[1][0], push[2][0]),
+            merge(turn_x[2], push[3][0]),
+            merge(*[p[1] for p in push]),
         ]
 
     def part(ref, *lead_index):
         return lambda start, n: ref.at[lead_index + (pl.ds(pl.multiple_of(start, 16), n),)]
 
-    x_steps = exchange(part(lead, 0), part(lead, 1))
+    x_steps = exchange(lambda start, n: piece, part(lead, 1))
     m_steps = exchange(part(m_ref, slice(None)), part(m_far, slice(None)))
     assert mv.count <= LINKS
     a, st = [[merge(*s) for s in zip(*lists)] for lists in (a_lists, st_lists)]
     d, e, u, m = d_steps, e_steps, u_steps, m_steps
     early = [
-        merge(mv.greet, own[0], u[0], e[0], own[1], a[0]),
+        merge(mv.greet, own[0], u[0], e[0], own[1]),
+        a[0],
+        None,
+        None,
         merge(u[1], e[1]),
         a[1],
-        merge(u[2], e[2]),
-        merge(u[3], a[2], a[3]),
+        merge(u[2], e[2], a[2], a[3]),
         e[3],
-        merge(u[4], e[4]),
+        merge(u[3], e[4]),
         e[5],
-        merge(a[4], e[6]),
-        merge(e[7], d[0]),
-        merge(u[5], e[8]),
-        merge(a[5], a[6], e[9]),
-        merge(e[10], d[1]),
-        d[2],
-        st[0],
+        e[6],
+        merge(e[7], a[4]),
+        u[4],
+        merge(a[5], d[0]),
+        e[8],
+        merge(e[9], u[5]),
     ]
     late = [
-        merge(m[0], d[3]),
+        merge(a[6], st[0]),
+        d[1],
+        m[0],
+        None,
+        None,
+        m[1],
+        merge(m[2], d[2]),
+        st[1],
+        m[3],
         a[7],
-        merge(m[1], st[1]),
-        d[4],
-        merge(m[2], st[2]),
+        merge(st[2], d[3]),
+        m[4],
+        st[3],
+        m[5],
         a[8],
-        merge(m[3], st[3]),
-        m[4],
         st[4],
-        m[5],
-        st[5],
-        m[6],
-        merge(st[6], a[9]),
     ]
-    return mv, early, x_steps, late
-
-
-def factor_loop(w, inv_s, up_s, l_ref, ticks):
+    last = [d[4], m[6], st[5], a[9], st[6]]
+    return mv, early, x_steps, e[10], late, last
+
+
+def factor_loop(w, inv_s, up_s, left, right, l_ref, ticks):
     width = w.shape[0]
     steps = width // NB
     if l_ref is not None:
@@ -487,15 +497,31 @@
         o = pl.multiple_of(k * NB, NB)
         here = pl.ds(o, NB)
         for i in range(0, len(ticks), 2):
-            pl.when(k == i // 2)(ticks[i])
+            if ticks[i] is not None:
+                pl.when(k == i // 2)(ticks[i])
         groups = [w[pl.ds(pl.multiple_of(o + 8 * i, 8), 8), here] for i in range(NB // 8)]
         up, inv = factor_diagonal(groups)
         for i in range(NB // 8):
             inv_s[8 * i : 8 * i + 8, :] = inv[i]
             up_s[8 * i : 8 * i + 8, :] = up[i]
         inverse = inv_s[...]
-        w[:, here] = dot_nt(w[:, here], inverse)
+        panel = dot3(w[:, here], inverse)
+
+        def clear(j, _):
+            w[here, pl.ds(pl.multiple_of(j * NB, NB), NB)] = jnp.zeros((NB, NB), F32)
+            return 0
+
+        lax.fori_loop(k + 1, steps, clear, 0)
+        w[:, here] = panel
         w[here, here] = inverse.T
+        hi, lo = split(w[:, here])
+        left[:, :NB] = hi
+        left[:, NB : 2 * NB] = hi
+        left[:, 2 * NB :] = lo
+        right[:, :NB] = hi
+        right[:, NB : 2 * NB] = lo
+        right[:, 2 * NB :] = hi
+        right[here, :] = jnp.zeros((NB, 3 * NB), BF16)
         if l_ref is not None:
             l_ref[here, here] = up_s[...].T
 
@@ -506,15 +532,15 @@
 
             lax.fori_loop(k + 1, steps, keep, 0)
         for i in range(1, len(ticks), 2):
-            pl.when(k == i // 2)(ticks[i])
+            if ticks[i] is not None:
+                pl.when(k == i // 2)(ticks[i])
 
         def update(j, _):
-            there = pl.ds(pl.multiple_of(j * NB, NB), NB)
-            w[here, there] = jnp.zeros((NB, NB), F32)
-            w[:, there] -= dot_nt(w[:, here], w[there, here])
+            there = pl.ds(pl.multiple_of(j * CUT, CUT), CUT)
+            w[:, there] -= dot16(left[...], right[there, :], NT)
             return 0
 
-        lax.fori_loop(k + 1, steps, update, 0)
+        lax.fori_loop((k + 1) * NB // CUT, width // CUT, update, 0)
         return 0
 
     lax.fori_loop(0, steps, step, 0)
@@ -532,40 +558,59 @@
             m_ref[:, end:, cut] = jnp.zeros((2, width - end, NB), BF16)
 
 
+def apply_upper(rows, m_ref, cut):
+    return dot16(rows, m_ref[0, : cut.stop, cut]) + dot16(rows, m_ref[1, : cut.stop, cut])
+
+
 def front_kernel(
     a_ref, keep_ref, raw, parent,
     m_ref, m_pivot, l_ref, g_ref, d_ref, st_ref, lead_out, far_out,
-    w, inv_s, up_s, u_ref, e_ref, lead, m_far, e_x, e_y, st_a, send_sems, recv_sems, local_sems,
+    w, inv_s, up_s, left, right, u_ref, e_ref, lead, m_far, piece, e_y, e_z, st_a,
+    send_sems, recv_sems, local_sems,
 ):
     width = a_ref.shape[0]
-    mv, early, swap, late = gather_program(
-        raw, parent, g_ref, d_ref, st_ref, m_ref, u_ref, e_ref, lead, m_far, e_x, e_y, st_a,
-        (send_sems, recv_sems, local_sems),
+    mv, early, swap, pivot_here, late, last = gather_program(
+        raw, parent, g_ref, d_ref, st_ref, m_ref, u_ref, e_ref, lead, m_far, piece, e_y, e_z,
+        st_a, (send_sems, recv_sems, local_sems),
     )
+    cuts = [slice(n, n + CUT) for n in range(0, width, CUT)]
     w[...] = a_ref[...]
-    factor_loop(w, inv_s, up_s, None, early)
+    factor_loop(w, inv_s, up_s, left, right, None, early)
     split_upper(w, m_ref)
-    for n in range(width // CUT):
-        end = (n + 1) * CUT
-        cut = slice(n * CUT, end)
-        rows = u_ref[:width, :end]
-        both = dot16(rows, m_ref[0, :end, cut]) + dot16(rows, m_ref[1, :end, cut])
+    mine = pl.ds(pl.multiple_of(mv.core * 512 + mv.at["x"] * 128 + mv.at["z"] * 32, 32), 32)
+    for cut in cuts:
+        both = apply_upper(u_ref[mine, : cut.stop], m_ref, cut)
+        piece[:, cut] = (both * keep_ref[mine, :1]).astype(BF16)
+    swap[0]()
+    for cut in cuts:
+        both = apply_upper(u_ref[:width, : cut.stop], m_ref, cut)
         lead[0, :, cut] = (both * keep_ref[:, :1]).astype(BF16)
-    for step in swap:
+    swap[1]()
+    pivot_here()
+
+    def subtract(i, cut, total):
+        w[cut.start :, cut] = total - dot16(lead[i, cut.start :, :], lead[i, cut, :], NT)
+
+    for n, cut in enumerate(cuts):
+        if n == 1:
+            swap[2]()
+        if n == 3:
+            swap[3]()
+        subtract(0, cut, e_ref[cut.start :, cut].astype(F32))
+    for step in swap[4:]:
         step()
     lead_copy = pltpu.make_async_copy(lead, lead_out, local_sems.at[14])
     far_copy = pltpu.make_async_copy(m_far, far_out, local_sems.at[15])
     lead_copy.start()
-    for n in range(width // CUT):
-        start = n * CUT
-        cut = slice(start, start + CUT)
-        total = e_ref[start:, cut].astype(F32)
-        for i in range(2):
-            total -= dot16(lead[i, start:, :], lead[i, cut, :], NT)
-        w[start:, cut] = total
-    factor_loop(w, inv_s, up_s, l_ref, late)
+    for cut in cuts:
+        subtract(1, cut, w[cut.start :, cut])
+    factor_loop(w, inv_s, up_s, left, right, l_ref, late)
+    split_upper(w, m_pivot)
+    for step in last[:3]:
+        step()
     far_copy.start()
-    split_upper(w, m_pivot)
+    for step in last[3:]:
+        step()
     mv.finish()
     lead_copy.wait()
     far_copy.wait()
@@ -595,10 +640,13 @@
             VM((width, width), F32),
             VM((NB, NB), F32),
             VM((NB, NB), F32),
+            VM((width, 3 * NB), BF16),
+            VM((width, 3 * NB), BF16),
             VM((16 * chunk, width), BF16),
             VM((width, width), BF16),
             VM((2, width, width), BF16),
             VM((2, width, width), BF16),
+            VM((32, width), BF16),
             VM((256, width), BF16),
             VM((64, width), BF16),
             VM((2, 512, 512), BF16),
@@ -620,189 +668,178 @@
     return -(-(TB + chunk - 16) // chunk)
 
 
-def spread_kernel(
-    chunk, tile_ref, have_ref, grp_ref, gathered, own_ref, far_ref, lead_ref, d_ref, st_ref,
-    s_ref, b_ref, buf, sem,
+def finish_kernel(
+    chunk, across, tile_ref, have_ref, flag_ref, gathered, own_hbm, far_hbm, lead_hbm, pivot_hbm,
+    l_ref, d_ref, st_ref, parent_ref, out_ref,
+    buf, sem, own, far, lead, pivot, load_sem, s_tile, b_tile, s_keep, f_keep,
 ):
-    t, g = pl.program_id(0), pl.program_id(1)
-    width = lead_ref.shape[1]
-    chunks = gathered.shape[1]
-    across = 2
+    t = pl.program_id(0)
+    tiles = pl.num_programs(0)
+    width = b_tile.shape[1]
     span = chunk_span(chunk)
-    slot = lax.rem(t * 2 + g, 2)
-
-    def copies(t, g, slot):
-        row = tile_ref[g * 6 + t] * TB
-        first = row // chunk
+    slot = lax.rem(t, 2)
+
+    def copies(t, slot):
         out = []
-        for i in range(span):
-            c = jnp.minimum(first + i, chunks - 1)
-            out.append(
-                pltpu.make_async_copy(
-                    gathered.at[g ^ grp_ref[0], c],
-                    buf.at[slot, pl.ds(i * chunk, chunk)],
-                    sem.at[slot, i],
+        for g in range(2):
+            first = tile_ref[g * tiles + t] * TB // chunk
+            for i in range(span):
+                c = jnp.minimum(first + i, gathered.shape[1] - 1)
+                out.append(
+                    pltpu.make_async_copy(
+                        gathered.at[g ^ flag_ref[2], c],
+                        buf.at[slot, g, pl.ds(i * chunk, chunk)],
+                        sem.at[slot, g, i],
+                    )
                 )
-            )
         return out
 
-    @pl.when((t == 0) & (g == 0))
-    def _():
-        for c in copies(t, g, slot):
+    loads = [
+        pltpu.make_async_copy(src, dst, load_sem.at[i])
+        for i, (src, dst) in enumerate(
+            ((own_hbm, own), (lead_hbm, lead), (far_hbm, far), (pivot_hbm, pivot))
+        )
+    ]
+
+    @pl.when(t == 0)
+    def _():
+        for c in copies(t, slot):
             c.start()
-
-    nxt = t * 2 + g + 1
-
-    @pl.when(nxt < 12)
-    def _():
-        for c in copies(nxt // 2, lax.rem(nxt, 2), 1 - slot):
+        for c in loads:
             c.start()
 
-    for c in copies(t, g, slot):
+    @pl.when(t + 1 < tiles)
+    def _():
+        for c in copies(t + 1, 1 - slot):
+            c.start()
+
+    for c in copies(t, slot):
         c.wait()
 
-    @pl.when((g == 0) & (t < across))
-    def _():
-        b_ref[...] = d_ref[...].astype(F32).T
-
-    @pl.when((g == 0) & (t >= across))
-    def _():
-        b_ref[...] = st_ref[...].astype(F32)
-
-    have = have_ref[g * 6 + t] != 0
-
-    @pl.when(jnp.logical_not(have))
-    def _():
-        s_ref[...] = jnp.zeros_like(s_ref)
-
-    row = tile_ref[g * 6 + t] * TB
-    rows = pl.ds(pl.multiple_of(lax.rem(row, chunk), 16), TB)
-
-    def fill(m_ref):
-        for n in range(width // CUT):
-            end = (n + 1) * CUT
-            cut = slice(n * CUT, end)
-            held = buf[slot, rows, :end]
-            part = dot16(held, m_ref[0, :end, cut]) + dot16(held, m_ref[1, :end, cut])
-            s_ref[:, cut] = part.astype(BF16)
-        b_ref[...] -= dot16(s_ref[...], lead_ref[g], NT)
-
-    pl.when(have & (g == 0))(lambda: fill(own_ref))
-    pl.when(have & (g == 1))(lambda: fill(far_ref))
-
-
-def spread(tiles, have, grp, gathered, m_own, m_far, lead_both, column_panel, stripe):
+    @pl.when(t < across)
+    def _():
+        b_tile[...] = d_ref[...].astype(F32).T
+
+    @pl.when(t >= across)
+    def _():
+        b_tile[...] = st_ref[...].astype(F32)
+
+    for g, m_ref in enumerate((own, far)):
+        have = have_ref[g * tiles + t] != 0
+        side = slice(g * width, (g + 1) * width)
+
+        @pl.when(t == 0)
+        def _():
+            loads[2 * g].wait()
+            if g == 0:
+                loads[1].wait()
+
+        @pl.when(jnp.logical_not(have))
+        def _():
+            s_tile[:, side] = jnp.zeros((TB, width), BF16)
+
+        @pl.when(have)
+        def _():
+            off = pl.multiple_of(lax.rem(tile_ref[g * tiles + t] * TB, chunk), 16)
+            for n in range(0, width, WIDE):
+                cut = slice(n, n + WIDE)
+                rows = buf[slot, g, pl.ds(off, TB), : n + WIDE]
+                s_tile[:, g * width + n : g * width + n + WIDE] = apply_upper(
+                    rows, m_ref, cut
+                ).astype(BF16)
+            b_tile[...] -= dot16(s_tile[:, side], lead[g], NT)
+
+    @pl.when(t == 0)
+    def _():
+        loads[3].wait()
+
+    b_hi, b_lo = split(b_tile[...])
+
+    def panel(n):
+        end = n + WIDE
+        hi, lo = pivot[0, :end, n:end], pivot[1, :end, n:end]
+        return dot16(b_hi[:, :end], hi) + dot16(b_hi[:, :end], lo) + dot16(b_lo[:, :end], hi)
+
+    first = flag_ref[0] != 0
+    lead_tile = (flag_ref[1] != 0) & (t < across + width // TB)
+    below = t >= across
+
+    @pl.when(jnp.logical_not(below))
+    def _():
+        here = pl.ds(pl.multiple_of(t * TB, TB), TB)
+        s_keep[here, :] = s_tile[...]
+        for n in range(0, width, WIDE):
+            f_keep[here, n : n + WIDE] = panel(n).astype(BF16)
+
+    @pl.when(below & first & lead_tile)
+    def _():
+        out_ref[...] = l_ref[...]
+
+    @pl.when(below & first & jnp.logical_not(lead_tile))
+    def _():
+        for n in range(0, width, WIDE):
+            out_ref[:, n : n + WIDE] = panel(n)
+
+    @pl.when(below & jnp.logical_not(first) & lead_tile)
+    def _():
+        out_ref[...] = jnp.zeros_like(out_ref)
+
+    @pl.when(below & jnp.logical_not(first) & jnp.logical_not(lead_tile))
+    def _():
+        f = jnp.concatenate([panel(n).astype(BF16) for n in range(0, width, WIDE)], axis=1)
+        out_ref[...] = parent_ref[...].astype(F32) - (
+            dot16(s_tile[...], s_keep[...], NT) + dot16(f, f_keep[...], NT)
+        )
+
+
+def finish(tiles, have, flags, gathered, m_own, m_far, lead_both, m_pivot, factor, panel, stripe, parent):
     chunk = gathered.shape[2]
     width = lead_both.shape[-1]
-    across = column_panel.shape[1] // TB
-    rows = column_panel.shape[1] + stripe.shape[0]
-    vmem = pl.BlockSpec(memory_space=VM)
+    cols = parent.shape[1]
+    across = cols // TB
+    lead = width // TB
+    grid = across + parent.shape[0] // TB
+    hbm = pl.BlockSpec(memory_space=pl.ANY)
+    pair = VM((2, width, width), BF16)
+    stripe_at = lambda t, *_: (jnp.maximum(t - across, 0), 0)
     return pl.pallas_call(
-        functools.partial(spread_kernel, chunk),
+        functools.partial(finish_kernel, chunk, across),
         grid_spec=pltpu.PrefetchScalarGridSpec(
             num_scalar_prefetch=3,
-            grid=(rows // TB, 2),
+            grid=(grid,),
             in_specs=[
-                pl.BlockSpec(memory_space=pl.ANY),
-                vmem,
-                vmem,
-                vmem,
-                pl.BlockSpec((width, TB), lambda t, g, *_: (0, jnp.minimum(t, across - 1))),
-                pl.BlockSpec((TB, width), lambda t, g, *_: (jnp.maximum(t - across, 0), 0)),
+                hbm,
+                hbm,
+                hbm,
+                hbm,
+                hbm,
+                pl.BlockSpec((TB, width), lambda t, *_: (jnp.clip(t - across, 0, lead - 1), 0)),
+                pl.BlockSpec((width, TB), lambda t, *_: (0, jnp.minimum(t, across - 1))),
+                pl.BlockSpec((TB, width), stripe_at),
+                pl.BlockSpec((TB, cols), stripe_at),
             ],
-            out_specs=[
-                pl.BlockSpec((TB, width), lambda t, g, *_: (t, g)),
-                pl.BlockSpec((TB, width), lambda t, g, *_: (t, 0)),
+            out_specs=pl.BlockSpec((TB, cols), stripe_at),
+            scratch_shapes=[
+                VM((2, 2, chunk_span(chunk) * chunk, width), BF16),
+                pltpu.SemaphoreType.DMA((2, 2, chunk_span(chunk))),
+                pair,
+                pair,
+                pair,
+                pair,
+                pltpu.SemaphoreType.DMA((4,)),
+                VM((TB, 2 * width), BF16),
+                VM((TB, width), F32),
+                VM((cols, 2 * width), BF16),
+                VM((cols, width), BF16),
             ],
-            scratch_shapes=[
-                VM((2, chunk_span(chunk) * chunk, width), BF16),
-                pltpu.SemaphoreType.DMA((2, chunk_span(chunk))),
-            ],
-        ),
-        out_shape=[
-            jax.ShapeDtypeStruct((rows, 2 * width), BF16),
-            jax.ShapeDtypeStruct((rows, width), F32),
-        ],
-        compiler_params=pltpu.CompilerParams(vmem_limit_bytes=52 * 2**20),
-        cost_estimate=pl.CostEstimate(
-            flops=35_000_000_000, bytes_accessed=40 * 2**20, transcendentals=0
-        ),
-        name="spread",
-    )(tiles, have, grp, gathered, m_own, m_far, lead_both, column_panel, stripe)
-
-
-def trailing_kernel(across, flag_ref, s_ref, b_ref, m_ref, l_ref, parent_ref, out_ref, s_keep, f_keep):
-    t = pl.program_id(0)
-    width = b_ref.shape[1]
-    b_hi, b_lo = split(b_ref[...])
-    panels = []
-    for n in range(width // CUT):
-        end = (n + 1) * CUT
-        cut = slice(n * CUT, end)
-        hi, lo = m_ref[0, :end, cut], m_ref[1, :end, cut]
-        panels.append(
-            dot16(b_hi[:, :end], hi) + dot16(b_hi[:, :end], lo) + dot16(b_lo[:, :end], hi)
-        )
-
-    @pl.when(t < across)
-    def _():
-        here = pl.ds(pl.multiple_of(t * TB, TB), TB)
-        s_keep[here, :] = s_ref[...]
-        for n in range(width // CUT):
-            f_keep[here, n * CUT : (n + 1) * CUT] = panels[n].astype(BF16)
-
-    @pl.when(t >= across)
-    def _():
-        first = flag_ref[0] != 0
-        pivot = (flag_ref[1] != 0) & (t < across + width // TB)
-
-        @pl.when(first & pivot)
-        def _():
-            out_ref[...] = l_ref[...]
-
-        @pl.when(first & jnp.logical_not(pivot))
-        def _():
-            for n in range(width // CUT):
-                out_ref[:, n * CUT : (n + 1) * CUT] = panels[n]
-
-        @pl.when(jnp.logical_not(first) & pivot)
-        def _():
-            out_ref[...] = jnp.zeros_like(out_ref)
-
-        @pl.when(jnp.logical_not(first) & jnp.logical_not(pivot))
-        def _():
-            f = jnp.concatenate([p.astype(BF16) for p in panels], axis=1)
-            out_ref[...] = parent_ref[...].astype(F32) - (
-                dot16(s_ref[...], s_keep[...], NT) + dot16(f, f_keep[...], NT)
-            )
-
-
-def trailing(flags, s_all, b_all, m_pivot, pivot_factor, parent):
-    width = b_all.shape[1]
-    cols = parent.shape[1]
-    across = cols // TB
-    tiles = parent.shape[0] // TB
-    lead = width // TB
-    return pl.pallas_call(
-        functools.partial(trailing_kernel, across),
-        grid_spec=pltpu.PrefetchScalarGridSpec(
-            num_scalar_prefetch=1,
-            grid=(across + tiles,),
-            in_specs=[
-                pl.BlockSpec((TB, 2 * width), lambda t, *_: (t, 0)),
-                pl.BlockSpec((TB, width), lambda t, *_: (t, 0)),
-                pl.BlockSpec(memory_space=VM),
-                pl.BlockSpec((TB, width), lambda t, *_: (jnp.clip(t - across, 0, lead - 1), 0)),
-                pl.BlockSpec((TB, cols), lambda t, *_: (jnp.maximum(t - across, 0), 0)),
-            ],
-            out_specs=pl.BlockSpec((TB, cols), lambda t, *_: (jnp.maximum(t - across, 0), 0)),
-            scratch_shapes=[VM((cols, 2 * width), BF16), VM((cols, width), BF16)],
         ),
         out_shape=jax.ShapeDtypeStruct(parent.shape, F32),
         compiler_params=pltpu.CompilerParams(vmem_limit_bytes=56 * 2**20),
-        cost_estimate=pl.CostEstimate(flops=35_000_000_000, bytes_accessed=40 * 2**20, transcendentals=0),
-        name="trailing",
-    )(flags, s_all, b_all, m_pivot, pivot_factor, parent)
+        cost_estimate=pl.CostEstimate(
+            flops=60_000_000_000, bytes_accessed=60 * 2**20, transcendentals=0
+        ),
+        name="finish",
+    )(tiles, have, flags, gathered, m_own, m_far, lead_both, m_pivot, factor, panel, stripe, parent)
 
 
 def locate(tile_map, parent_tiles):
@@ -844,11 +881,11 @@
         tiles.append(inverse[wanted_tiles])
         have.append(present[wanted_tiles].astype(jnp.int32))
     tiles, have = jnp.concatenate(tiles), jnp.concatenate(have)
-    s_all, b_all = spread(
-        tiles, have, grp[None], gathered, m_own, m_far, lead_both, column_panel, stripe
+    flags = jnp.stack([block == 0, row == 0, grp == 1]).astype(jnp.int32)
+    return finish(
+        tiles, have, flags, gathered, m_own, m_far, lead_both, m_pivot, pivot_factor,
+        column_panel, stripe, parent_front,
     )
-    flags = jnp.stack([block == 0, row == 0]).astype(jnp.int32)
-    return trailing(flags, s_all, b_all, m_pivot, pivot_factor, parent_front)
 
 
 def solution(mesh):

time: 343 us -> 328 us (0.956)
  the two profiles are of different devices: /device:TPU:49 before, /device:TPU:10 now
where the time goes in v2:
time: 328 us
  Pallas kernels  320 us (98%)
  local copies, waits for them, and re-layouts  4.49 us (1%)
    pallas_call x1, Pallas kernels, front(): pl.pallas_call(front_kernel, out_shape=[pair, pair, jax.ShapeDtypeStruct(...  244 us
    pallas_call x1, Pallas kernels, finish(): pl.pallas_call(functools.partial(finish_kernel, chunk, across), grid_spec...  75.8 us

profile of v2, /device:TPU:10, one launch (start us, length us, event | category | flops | bytes accessed | tf_op | source)
XLA Modules:
  0.0 327.7 jit_solution(3439308627787828632)
XLA Ops:
  0.0 0.6 add_convert_fusion.1.flag_ref
  0.6 0.1 fusion.2
  0.6 0.7 rev.3
  1.3 0.7 broadcast_select_fusion
  2.0 0.1 fusion
  2.1 0.1 select_reduce_fusion
  2.2 0.6 gather_fusion.3
  2.9 0.7 gather_fusion.2
  3.5 0.6 add_convert_fusion.have_ref
  4.1 0.6 gather_fusion.1
  4.7 0.6 gather_fusion
  5.4 0.6 pad_add_fusion.tile_ref
  6.0 0.1 broadcast_bitcast_fusion
  6.1 0.2 broadcast_in_dim.41.keep_ref
  6.3 0.0 copy-start
  6.3 0.9 copy-done
  7.2 244.5 %front.1 = (bf16[2,1024,1024]{2,1,0:T(8,128)(2,1)}, bf16[2,1024,1024]{2,1,0:T(8,128)(2,1)}, f32[1024,1024]{1,0:T(8,128)}, bf16[2,4,2,2,4,112,1024]{6,5,4,3,2,1,0...) custom-call(f32[1024,1024]{1,0:T(8,128)} %bitcast.23, ...), custom_call_target="tpu_custom_call" | custom-call | flops 120000004096 | bytes 16777216 | tf_op jit(solution)/shard_map/front/pallas_call | solution.py:625
  251.7 75.8 %finish.1 = f32[2048,1024]{1,0:T(8,128)} custom-call(s32[12]{0:T(128)} %pad_add_fusion.tile_ref, s32[12]{0:T(128)} %add_convert_fusion.have_ref, s32[3]{0:T(128)} %add_convert_fusion.1.flag_ref, bf16[2,64,112,1024]{3,2,1,0:T(8,128)(2,1)} %bitcast.24, bf16[2,1024,1024]{2,1,0:T(8,128)(2,1)} %get-tuple-element.14.own_hbm, ...), custom_call_target="tpu_custom_call" | custom-call | flops 60000002048 | bytes 62914560 | tf_op jit(solution)/shard_map/finish/pallas_call | solution.py:805
  (6 shorter events, 0.0 us)
Async XLA Ops:
  6.3 0.9 copy-start

commit v3 on v2

--- a/solution.py
+++ b/solution.py
@@ -135,7 +135,7 @@
 
 
 AXES = ("x", "y", "z")
-CUTS = ((0, 384), (384, 256), (640, 384))
+CUTS = ((0, 48), (48, 32), (80, 32))
 ORDERS = (("y", "z", "x"), ("z", "x", "y"), ("x", "y", "z"))
 LINKS = 144
 
@@ -210,6 +210,24 @@
             passed.wait_recv()
 
         return [guard(when, f) for f in (first, second, third)]
+
+    def line(self, axis, region, when=None):
+        here = self.at[axis]
+        copies = [
+            self.make(region(here), region(here), self.device(axis, self.shifted(axis, by)))
+            for by in (1, 3, 2)
+        ]
+        self.sent += [(c, when) for c in copies]
+
+        def first():
+            for c in copies:
+                c.start()
+
+        def second():
+            for c in copies:
+                c.wait_recv()
+
+        return [guard(when, first), guard(when, second)]
 
     def scatter(self, axis, source, target, when=None):
         here = self.at[axis]
@@ -294,7 +312,7 @@
         gy = (place["y"] // 2, lax.rem(place["y"], 2)) if "y" in place else (slice(None),) * 2
         px = place.get("x", slice(None))
         pz = place.get("z", slice(None))
-        return g_ref.at[gy[0], px, core, gy[1], pz, :, pl.ds(*cut)]
+        return g_ref.at[gy[0], px, core, gy[1], pz, pl.ds(*cut)]
 
     own = local(raw, g_ref.at[y // 2, x, core, lax.rem(y, 2), z])
     a_lists = []
@@ -329,47 +347,40 @@
         push[1],
     ]
 
-    e_row = y * 256 + z * 64 + x * 16
-    cut_x = lambda k: rows_of(e_ref, y * 256 + z * 64 + k * 16, 16)
     cut_z = lambda k: rows_of(e_ref, y * 256 + k * 64, 64)
     cut_y = lambda k: rows_of(e_ref, k * 256, 256)
     on_y = lead_core & (x == 0) & (z == 0)
     on_z = lead_core & (x == 0)
     loc_y = local(parent.at[pl.ds(0, 256)], e_y, on_y & (y == 0))
     loc_z = local(e_y.at[pl.ds(0, 64)], e_z, on_z & (z == 0))
-    loc_x = local(e_z.at[pl.ds(0, 16)], rows_of(e_ref, e_row, 16), on_z)
+    loc_x = local(e_z, cut_z(z), on_z)
     hand_y = mv.scatter("y", lambda k: rows_of(parent, k * 256, 256), lambda k: e_y, on_y)
     hand_z = mv.scatter("z", lambda k: e_y.at[pl.ds(64 * k, 64)], lambda k: e_z, on_z)
-    hand_x = mv.scatter("x", lambda k: e_z.at[pl.ds(16 * k, 16)], cut_x, lead_core)
-    turn_x = mv.ring("x", cut_x, lead_core)
-    turn_z = mv.ring("z", cut_z, lead_core)
-    turn_y = mv.ring("y", cut_y, lead_core)
+    hand_x = mv.scatter("x", lambda k: e_z, lambda k: cut_z(z), lead_core)
+    turn_z = mv.line("z", cut_z, lead_core)
+    turn_y = mv.line("y", cut_y, lead_core)
     push = mv.push(e_ref, lead_core, core == 1)
     e_steps = [
         merge(loc_y[0], hand_y[0]),
         merge(loc_y[1], hand_y[1], loc_z[0], hand_z[0]),
         merge(loc_z[1], hand_z[1], loc_x[0], hand_x[0]),
-        merge(loc_x[1], hand_x[1], turn_x[0]),
-        turn_x[1],
-        merge(turn_x[2], turn_z[0]),
-        turn_z[1],
-        merge(turn_z[2], turn_y[0]),
-        turn_y[1],
-        merge(turn_y[2], push[0]),
+        merge(loc_x[1], hand_x[1], turn_z[0]),
+        merge(turn_z[1], turn_y[0]),
+        merge(turn_y[1], push[0]),
         push[1],
     ]
 
     st_lists = []
-    for i, ((a, b), cut) in enumerate(((("z", "y"), (0, 512)), (("y", "z"), (512, 512)))):
-        wide = lambda k, cut=cut: rows_of(st_ref, k * 512, 512, cut)
-        wide_source = lambda k, cut=cut: rows_of(parent, k * 512, 512, cut)
-        fine = lambda k, a=a, cut=cut: rows_of(st_ref, mv.at[a] * 512 + k * 128, 128, cut)
+    for i, (a, b) in enumerate((("z", "y"), ("y", "z"))):
+        wide = lambda k, i=i: rows_of(st_ref, k * 512 + i * 256, 256)
+        wide_source = lambda k, i=i: rows_of(parent, k * 512 + i * 256, 256)
+        fine = lambda k, a=a, i=i: rows_of(st_ref, mv.at[a] * 512 + i * 256 + k * 64, 64)
         held = st_a.at[i]
         line = mv.at[b] == 0
         loc_a = local(wide_source(0), held, line & (mv.at[a] == 0))
-        loc_b = local(held.at[pl.ds(0, 128)], fine(0), line)
+        loc_b = local(held.at[pl.ds(0, 64)], fine(0), line)
         hand_a = mv.scatter(a, wide_source, lambda k: held, line)
-        hand_b = mv.scatter(b, lambda k: held.at[pl.ds(k * 128, 128)], fine)
+        hand_b = mv.scatter(b, lambda k: held.at[pl.ds(k * 64, 64)], fine)
         turn_b = mv.ring(b, fine)
         turn_a = mv.ring(a, wide)
         st_lists.append(
@@ -390,7 +401,7 @@
     chunk_z = lambda k: rows_of(u_ref, base + (y_lo * 4 + k) * size, size)
     u_own = local(raw, chunk_z(z), x == 0)
     u_hand = mv.scatter("x", lambda k: raw, lambda k: chunk_z(z))
-    u_turn = mv.ring("z", chunk_z)
+    u_turn = mv.line("z", chunk_z)
     full = 8 * size
     rest = e_ref.shape[0] - full
     beside = {"col": (1 - y_lo) * 4 + z}
@@ -405,9 +416,8 @@
     u_steps = [
         merge(u_own[0], u_hand[0]),
         merge(u_own[1], u_hand[1], u_turn[0]),
-        u_turn[1],
         merge(
-            u_turn[2],
+            u_turn[1],
             guard(lead_core, swap.start),
             guard((core == 1) & (y_lo == 0), slide.start),
         ),
@@ -420,15 +430,24 @@
         merge(push_head[1], push_tail[1]),
     ]
 
-    def exchange(mine, theirs):
+    def exchange(mine, theirs, direct):
         start = core * 512 + x * 128 + z * 32
         across = mv.make(mine(start, 32), theirs(start, 32), mv.device("y", mv.shifted("y", 2)))
         mv.sent.append((across, None))
-        turn_z = mv.ring("z", lambda k: theirs(core * 512 + x * 128 + k * 32, 32))
-        turn_x = mv.ring("x", lambda k: theirs(core * 512 + k * 128, 128))
+        turn = mv.line if direct else mv.ring
+        turn_z = turn("z", lambda k: theirs(core * 512 + x * 128 + k * 32, 32))
+        turn_x = turn("x", lambda k: theirs(core * 512 + k * 128, 128))
         push = [
             mv.push(theirs(core * 512 + mv.shifted("x", by) * 128, 128)) for by in (0, 1, 3, 2)
         ]
+        if direct:
+            return [
+                across.start,
+                merge(across.wait_recv, turn_z[0]),
+                merge(turn_z[1], turn_x[0], push[0][0]),
+                merge(turn_x[1], push[1][0], push[2][0], push[3][0]),
+                merge(*[p[1] for p in push]),
+            ]
         return [
             across.start,
             merge(across.wait_recv, turn_z[0]),
@@ -442,8 +461,8 @@
     def part(ref, *lead_index):
         return lambda start, n: ref.at[lead_index + (pl.ds(pl.multiple_of(start, 16), n),)]
 
-    x_steps = exchange(lambda start, n: piece, part(lead, 1))
-    m_steps = exchange(part(m_ref, slice(None)), part(m_far, slice(None)))
+    x_steps = exchange(lambda start, n: piece, part(lead, 1), True)
+    m_steps = exchange(part(m_ref, slice(None)), part(m_far, slice(None)), False)
     assert mv.count <= LINKS
     a, st = [[merge(*s) for s in zip(*lists)] for lists in (a_lists, st_lists)]
     d, e, u, m = d_steps, e_steps, u_steps, m_steps
@@ -452,18 +471,18 @@
         a[0],
         None,
         None,
+        None,
         merge(u[1], e[1]),
         a[1],
-        merge(u[2], e[2], a[2], a[3]),
+        e[2],
+        merge(a[2], a[3]),
         e[3],
-        merge(u[3], e[4]),
-        e[5],
-        e[6],
-        merge(e[7], a[4]),
-        u[4],
-        merge(a[5], d[0]),
-        e[8],
-        merge(e[9], u[5]),
+        u[2],
+        e[4],
+        a[4],
+        d[0],
+        merge(u[3], a[5]),
+        merge(e[5], u[4]),
     ]
     late = [
         merge(a[6], st[0]),
@@ -484,7 +503,7 @@
         st[4],
     ]
     last = [d[4], m[6], st[5], a[9], st[6]]
-    return mv, early, x_steps, e[10], late, last
+    return mv, early, x_steps, e[6], late, last
 
 
 def factor_loop(w, inv_s, up_s, left, right, l_ref, ticks):
@@ -594,10 +613,8 @@
     for n, cut in enumerate(cuts):
         if n == 1:
             swap[2]()
-        if n == 3:
-            swap[3]()
         subtract(0, cut, e_ref[cut.start :, cut].astype(F32))
-    for step in swap[4:]:
+    for step in swap[3:]:
         step()
     lead_copy = pltpu.make_async_copy(lead, lead_out, local_sems.at[14])
     far_copy = pltpu.make_async_copy(m_far, far_out, local_sems.at[15])
@@ -649,7 +666,7 @@
             VM((32, width), BF16),
             VM((256, width), BF16),
             VM((64, width), BF16),
-            VM((2, 512, 512), BF16),
+            VM((2, 256, width), BF16),
             pltpu.SemaphoreType.DMA((LINKS,)),
             pltpu.SemaphoreType.DMA((LINKS,)),
             pltpu.SemaphoreType.DMA((16,)),

time: 328 us -> 307 us (0.936)
  the two profiles are of different devices: /device:TPU:10 before, /device:TPU:11 now
where the time goes in v3:
time: 307 us
  Pallas kernels  299 us (97%)
  local copies, waits for them, and re-layouts  4.49 us (1%)
    pallas_call x1, Pallas kernels, front(): pl.pallas_call(front_kernel, out_shape=[pair, pair, jax.ShapeDtypeStruct(...  235 us
    pallas_call x1, Pallas kernels, finish(): pl.pallas_call(functools.partial(finish_kernel, chunk, across), grid_spec...  64.6 us

profile of v3, /device:TPU:11, one launch (start us, length us, event | category | flops | bytes accessed | tf_op | source)
XLA Modules:
  0.0 306.6 jit_solution(16446594798916404195)
XLA Ops:
  0.0 0.6 add_convert_fusion.1.flag_ref
  0.6 0.1 fusion.2
  0.6 0.7 rev.3
  1.3 0.7 broadcast_select_fusion
  2.0 0.1 fusion
  2.1 0.1 select_reduce_fusion
  2.2 0.6 gather_fusion.3
  2.9 0.7 gather_fusion.2
  3.5 0.6 add_convert_fusion.have_ref
  4.1 0.6 gather_fusion.1
  4.7 0.6 gather_fusion
  5.4 0.6 pad_add_fusion.tile_ref
  6.0 0.1 broadcast_bitcast_fusion
  6.1 0.2 broadcast_in_dim.41.keep_ref
  6.3 0.0 copy-start
  6.3 0.9 copy-done
  7.2 234.7 %front.1 = (bf16[2,1024,1024]{2,1,0:T(8,128)(2,1)}, bf16[2,1024,1024]{2,1,0:T(8,128)(2,1)}, f32[1024,1024]{1,0:T(8,128)}, bf16[2,4,2,2,4,112,1024]{6,5,4,3,2,1,0...) custom-call(f32[1024,1024]{1,0:T(8,128)} %bitcast.23, ...), custom_call_target="tpu_custom_call" | custom-call | flops 120000004096 | bytes 16777216 | tf_op jit(solution)/shard_map/front/pallas_call | solution.py:642
  241.9 64.6 %finish.1 = f32[2048,1024]{1,0:T(8,128)} custom-call(s32[12]{0:T(128)} %pad_add_fusion.tile_ref, s32[12]{0:T(128)} %add_convert_fusion.have_ref, s32[3]{0:T(128)} %add_convert_fusion.1.flag_ref, bf16[2,64,112,1024]{3,2,1,0:T(8,128)(2,1)} %bitcast.24, bf16[2,1024,1024]{2,1,0:T(8,128)(2,1)} %get-tuple-element.14.own_hbm, ...), custom_call_target="tpu_custom_call" | custom-call | flops 60000002048 | bytes 62914560 | tf_op jit(solution)/shard_map/finish/pallas_call | solution.py:822
  (6 shorter events, 0.0 us)
Async XLA Ops:
  6.3 0.9 copy-start
